TPU v7x, 32 devices: a whole 2x2x4 slice. The times are simulated.
32 devices in a mesh: rows: 4 (over z), cols: 2 (over x), rep: 4 (over y, core).
Axes of the slice: x: 2, y: 2, z: 4, core: 2. Of those that a mesh axis runs over, the one named last changes fastest.
Arguments:
- feature_map: bfloat16 [4, 32, 32, 384], P('rep', 'rows', 'cols'), may hold values from -6 to 6
- dw_kernel: float32 [7, 7, 384], replicated, may hold values from -0.875 to 0.875
- dw_bias: float32 [384], replicated, may hold values from -3 to 3
- layer_norm_gain: float32 [384], replicated, may hold values from 0.5 to 1.5
- layer_norm_bias: float32 [384], replicated, may hold values from -3 to 3
- w_expand: bfloat16 [384, 1536], replicated, may hold values from -0.3125 to 0.3125
- b_expand: float32 [1536], replicated, may hold values from -3 to 3
- w_reduce: bfloat16 [1536, 384], replicated, may hold values from -0.15625 to 0.15625
- b_reduce: float32 [384], replicated, may hold values from -3 to 3
- layer_scale: float32 [384], replicated, may hold values from 0.5 to 1.5
- cotangent: bfloat16 [4, 32, 32, 384], P('rep', 'rows', 'cols'), may hold values from -6 to 6
Outputs:
- block_out: bfloat16 [4, 32, 32, 384], P('rep', 'rows', 'cols')
- grad_input: bfloat16 [4, 32, 32, 384], P('rep', 'rows', 'cols')
- grad_expand: float32 [384, 1536], P('rep', ('rows', 'cols'))
- grad_reduce_t: float32 [384, 1536], P('rep', ('rows', 'cols'))
- grad_kernel: float32 [7, 7, 384], replicated
- grad_vectors: float32 [5, 384], replicated
- grad_bexp: float32 [1536], replicated
All inputs are finite; a program needn't handle non-finite values.
Results may differ from a plain program's by a relative error of at most 0.0062.
Values may be sent and summed in bfloat16 or wider, within the bound.
A program may use at most 64 MiB of HBM per device.

v0:
```python
import jax
import jax.numpy as jnp
from jax import lax
from jax.sharding import PartitionSpec as P

EPS = 1e-06
INV_ROOT_TWO = 0.7071067811865476
INV_ROOT_TWO_PI = 0.3989422804014327


def extended(cells, sides, width):
    for axis, dim in sides:
        count = lax.axis_size(axis)
        ends = count - 1
        head = lax.slice_in_dim(cells, 0, width, axis=dim)
        tail = lax.slice_in_dim(cells, cells.shape[dim] - width, cells.shape[dim], axis=dim)
        cells = jnp.concatenate(
            [
                lax.ppermute(tail, axis, [(i, (i + 1) % count) for i in range(ends)]),
                cells,
                lax.ppermute(head, axis, [((i + 1) % count, i) for i in range(ends)]),
            ],
            axis=dim,
        )
    return cells


def depthwise(padded, kernel, height, width):
    total = jnp.zeros((height, width, padded.shape[-1]), jnp.float32)
    for i in range(7):
        for j in range(7):
            total = total + kernel[i, j] * padded[i : i + height, j : j + width].astype(jnp.float32)
    return total


def front_pass(
    xpad,
    gout,
    dw_kernel,
    dw_bias,
    layer_norm_gain,
    layer_norm_bias,
    w_expand,
    b_expand,
    w_reduce,
    b_reduce,
    layer_scale,
    height,
    width,
):
    chans = xpad.shape[-1]
    conv = depthwise(xpad, dw_kernel, height, width) + dw_bias
    flat = conv.reshape(-1, chans)
    centered_input = flat - jnp.mean(flat, axis=-1, keepdims=True)
    inverse_deviation = lax.rsqrt(
        jnp.mean(centered_input * centered_input, axis=-1, keepdims=True) + EPS
    )
    standardized_input = centered_input * inverse_deviation
    normalized_rows = (standardized_input * layer_norm_gain + layer_norm_bias).astype(jnp.bfloat16)
    pre = jnp.dot(normalized_rows, w_expand, preferred_element_type=jnp.float32) + b_expand
    cdf = 0.5 * (1.0 + lax.erf(pre * INV_ROOT_TWO))
    act = (pre * cdf).astype(jnp.bfloat16)
    branch = jnp.dot(act, w_reduce, preferred_element_type=jnp.float32) + b_reduce
    inner = xpad[3 : 3 + height, 3 : 3 + width].reshape(-1, chans).astype(jnp.float32)
    block_out = (inner + layer_scale * branch).astype(jnp.bfloat16).reshape(height, width, chans)
    grad = gout.reshape(-1, chans).astype(jnp.float32)
    scaled = grad * layer_scale
    g_branch = scaled.astype(jnp.bfloat16)
    g_scale = jnp.sum(grad * branch, axis=0)
    g_breduce = jnp.sum(scaled, axis=0)
    grad_reduce_t = lax.dot_general(
        g_branch, act, (((0,), (0,)), ((), ())), preferred_element_type=jnp.float32
    )
    g_act = lax.dot_general(
        g_branch, w_reduce, (((1,), (1,)), ((), ())), preferred_element_type=jnp.float32
    )
    pdf = jnp.exp(-0.5 * pre * pre) * INV_ROOT_TWO_PI
    g_pre = g_act * (cdf + pre * pdf)
    g_bexp = jnp.sum(g_pre, axis=0)
    g_pre_b = g_pre.astype(jnp.bfloat16)
    grad_expand = lax.dot_general(
        normalized_rows, g_pre_b, (((0,), (0,)), ((), ())), preferred_element_type=jnp.float32
    )
    grad_normalized = lax.dot_general(
        g_pre_b, w_expand, (((1,), (1,)), ((), ())), preferred_element_type=jnp.float32
    )
    grad_norm_gain = jnp.sum(grad_normalized * standardized_input, axis=0)
    g_lnbias = jnp.sum(grad_normalized, axis=0)
    scaled_grad_input = grad_normalized * layer_norm_gain
    grad_convolution = inverse_deviation * (
        scaled_grad_input
        - jnp.mean(scaled_grad_input, axis=-1, keepdims=True)
        - standardized_input
        * jnp.mean(scaled_grad_input * standardized_input, axis=-1, keepdims=True)
    )
    g_dwbias = jnp.sum(grad_convolution, axis=0)
    vectors = jnp.stack([g_dwbias, grad_norm_gain, g_lnbias, g_breduce, g_scale])
    return (
        block_out,
        grad_convolution.reshape(height, width, chans),
        grad_expand,
        grad_reduce_t,
        vectors,
        g_bexp,
    )


def back_pass(gpad, xpad, gout, dw_kernel, height, width):
    inner = gpad[3 : 3 + height, 3 : 3 + width]
    grad_in = gout.astype(jnp.float32)
    kernel_rows = []
    for i in range(7):
        row_terms = []
        for j in range(7):
            part = xpad[i : i + height, j : j + width].astype(jnp.float32)
            row_terms.append(jnp.sum(inner * part, axis=(0, 1)))
            grad_in = (
                grad_in + dw_kernel[i, j] * gpad[6 - i : 6 - i + height, 6 - j : 6 - j + width]
            )
        kernel_rows.append(jnp.stack(row_terms))
    return (grad_in.astype(jnp.bfloat16), jnp.stack(kernel_rows))


def per_device(
    feature_map,
    dw_kernel,
    dw_bias,
    layer_norm_gain,
    layer_norm_bias,
    w_expand,
    b_expand,
    w_reduce,
    b_reduce,
    layer_scale,
    cotangent,
):
    height, width = (feature_map.shape[1], feature_map.shape[2])
    xpad = extended(feature_map, (("rows", 1), ("cols", 2)), 3)[0]
    gout = cotangent[0]
    block_out, grad_convolution, gexp, gred, vectors, gbexp = front_pass(
        xpad,
        gout,
        dw_kernel,
        dw_bias,
        layer_norm_gain,
        layer_norm_bias,
        w_expand,
        b_expand,
        w_reduce,
        b_reduce,
        layer_scale,
        height,
        width,
    )
    stacked = jnp.stack([gexp, gred])
    gpad = extended(grad_convolution, (("rows", 0), ("cols", 1)), 3)
    grad_in, gker = back_pass(gpad, xpad, gout, dw_kernel, height, width)
    partial_sum = lax.psum_scatter(stacked, "rep", scatter_dimension=1, tiled=True)
    summed = lax.psum_scatter(partial_sum, ("rows", "cols"), scatter_dimension=2, tiled=True)
    gker, vectors, gbexp = lax.psum((gker, vectors, gbexp), ("rows", "cols", "rep"))
    count = lax.axis_size("rows") * height * lax.axis_size("cols") * width * lax.axis_size("rep")
    scale = 1.0 / jnp.sqrt(jnp.float32(count))
    return (
        block_out[None],
        grad_in[None],
        summed[0] * scale,
        summed[1] * scale,
        gker * scale,
        vectors * scale,
        gbexp * scale,
    )


def solution(mesh):
    in_specs = (
        P("rep", "rows", "cols", None),
        P(),
        P(),
        P(),
        P(),
        P(),
        P(),
        P(),
        P(),
        P(),
        P("rep", "rows", "cols", None),
    )
    out_specs = (
        P("rep", "rows", "cols", None),
        P("rep", "rows", "cols", None),
        P("rep", ("rows", "cols")),
        P("rep", ("rows", "cols")),
        P(),
        P(),
        P(),
    )
    return jax.shard_map(
        per_device, mesh=mesh, in_specs=in_specs, out_specs=out_specs, check_vma=False
    )
```

profile of v0, /device:TPU:0, one launch (start us, length us, event | category | flops | bytes accessed | tf_op | source)
XLA Modules:
  0.0 200.0 jit_solution(14035500917182496346)
XLA Ops:
  8.1 0.9 fusion.176
  9.0 1.3 collective-permute-start.1
  10.2 5.6 %collective-permute-start = (bf16[1,3,16,384]{3,2,1,0:T(8,128)(2,1)S(1)}, bf16[1,3,16,384]{3,2,1,0:T(8,128)(2,1)S(1)}, u32[]{:S(2)}, u32[]{:S(2)}) collective-permute-start(bf16[1,3,16,384]{3,2,1,0:T(8,128)(2,1)S(1)} %get-tuple-element.129), channel_id=1, source_target_pairs={{0,8},{8,16},{16,24},{1,9},{9,17},{17,25},{2,10},{10,18},{18,26},{... | collective-permute-start | bytes 110600 | tf_op jit(solution)/shard_map/ppermute | solution.py:19
  15.8 1.3 slice_reduce_fusion.47
  17.1 1.2 slice_reduce_fusion.48
  18.3 0.9 constant_dynamic-update-slice_fusion.1
  19.3 3.8 %collective-permute-start.2 = (bf16[1,14,3,384]{3,2,1,0:T(4,128)(2,1)S(1)}, bf16[1,14,3,384]{3,2,1,0:T(4,128)(2,1)S(1)}, u32[]{:S(2)}, u32[]{:S(2)}) collective-permute-start(bf16[1,14,3,384]{3,2,1,0:T(4,128)(2,1)S(1)} %get-tuple-element.125), channel_id=1, source_target_pairs={{0,4},{1,5},{2,6},{3,7},{8,12},{9,13},{10,14},{11,15},{16,20},{17,... | collective-permute-start | bytes 96776 | tf_op jit(solution)/shard_map/ppermute | solution.py:19
  23.1 1.3 collective-permute-start.3
  24.4 1.0 slice_reduce_fusion.46
  25.4 3.6 %collective-permute-done.3 = bf16[1,14,3,384]{3,2,1,0:T(4,128)(2,1)S(1)} collective-permute-done((bf16[1,14,3,384]{3,2,1,0:T(4,128)(2,1)S(1)}, bf16[1,14,3,384]{3,2,1,0:T(4,128)(2,1)S(1)}, u32[]{:S(2)}, u32[]{:S(2)}) %collective-permute-start.3) | collective-permute-done | bytes 32288 | tf_op jit(solution)/shard_map/ppermute | solution.py:21
  29.2 1.6 fusion.171
  31.8 0.8 copy-done.1
  32.6 1.0 fusion.161
  34.2 0.6 fusion.177
  35.2 2.4 %pad_maximum_fusion = f32[2,384,1536]{2,1,0:T(8,128)} fusion(f32[1,384,1536]{2,1,0:T(8,128)S(1)} %convolution_bitcast_fusion, f32[1,384,1536]{2,1,0:T(8,128)S(1)} %convolution_bitcast_fusion.1), kind=kLoop, calls=%fused_computation | loop fusion | flops 1179648 | bytes 9437184 | tf_op jit(solution)/shard_map/stack | solution.py:155
  37.7 0.6 multiply_reduce_fusion
  40.5 0.6 copy-done.3
  41.2 44.8 %reduce-scatter.5.cloned.1.call-done = f32[2,96,1536]{2,1,0:T(8,128)} async-done(((f32[2,384,1536]{2,1,0:T(8,128)}), f32[2,96,1536]{2,1,0:T(8,128)}) %reduce-scatter.5.cloned.1.call-update) | async-done | bytes 1179664 | tf_op jit(solution)/shard_map/reduce_scatter | solution.py:158
  86.0 2.5 %copy.18 = f32[2,96,1536]{1,0,2:T(2,128)S(1)} copy(f32[2,96,1536]{2,1,0:T(8,128)} %reduce-scatter.5.cloned.1.call-done) | data formatting | bytes 2359296
  88.5 2.1 %reshape.88 = f32[1536,192]{1,0:T(8,128)} reshape(f32[1536,2,96]{2,1,0:T(2,128)S(1)} %bitcast.128) | data formatting | bytes 2359296
  90.7 1.3 collective-permute-start.5
  92.0 4.5 %collective-permute-start.4 = (f32[3,16,384]{2,1,0:T(8,128)S(1)}, f32[3,16,384]{2,1,0:T(8,128)S(1)}, u32[]{:S(2)}, u32[]{:S(2)}) collective-permute-start(f32[3,16,384]{2,1,0:T(8,128)S(1)} %bitcast.131), channel_id=1, source_target_pairs={{0,8},{8,16},{16,24},{1,9},{9,17},{17,25},{2,10},{10,18},{18,26},{... | collective-permute-start | bytes 221192 | tf_op jit(solution)/shard_map/ppermute | solution.py:19
  96.6 40.1 %all-reduce = (f32[5,384]{1,0:T(8,128)S(1)}, f32[1536]{0:T(1024)S(1)}) all-reduce(f32[5,384]{1,0:T(8,128)S(1)} %stack.291, f32[1536]{0:T(1024)S(1)} %get-tuple-element.133), channel_id=1, replica_groups=mesh['rows'=4,'cols'=2,'rep'=4] {'rows','cols','rep'}, use_global_device_ids=true, to_apply=%region_61.0 | all-reduce | flops 3456 | bytes 27648 | tf_op jit(solution)/shard_map/psum | solution.py:160
  136.7 0.6 broadcast_multiply_fusion.1
  137.3 0.6 broadcast_multiply_fusion.2
  137.9 1.3 collective-permute-start.6
  139.2 4.6 %collective-permute-start.7 = (f32[14,3,384]{2,1,0:T(4,128)S(1)}, f32[14,3,384]{2,1,0:T(4,128)S(1)}, u32[]{:S(2)}, u32[]{:S(2)}) collective-permute-start(f32[14,3,384]{2,1,0:T(4,128)S(1)} %get-tuple-element.118), channel_id=1, source_target_pairs={{0,4},{1,5},{2,6},{3,7},{8,12},{9,13},{10,14},{11,15},{16,20},{17,... | collective-permute-start | bytes 193544 | tf_op jit(solution)/shard_map/ppermute | solution.py:19
  143.8 43.0 %all-reduce.3.cloned.1.call-done = f32[7,7,384]{2,1,0:T(8,128)} async-done(((f32[7,7,384]{2,1,0:T(8,128)}), f32[7,7,384]{2,1,0:T(8,128)}) %all-reduce.3.cloned.1.call-update) | async-done | bytes 75280 | tf_op jit(solution)/shard_map/psum | solution.py:160
  186.8 1.5 broadcast_multiply_fusion
  188.4 2.0 fusion.169
  190.4 1.1 reshape.89
  191.9 0.7 multiply_bitcast_fusion
  (127 shorter events, 4.5 us)
Async XLA Ops:
  8.0 23.3 %copy-start = (bf16[384,1536]{1,0:T(8,128)(2,1)S(1)}, bf16[384,1536]{1,0:T(8,128)(2,1)}, u32[]{:S(2)}) copy-start(bf16[384,1536]{1,0:T(8,128)(2,1)} %param.16) | copy-start | bytes 3538948
  8.0 21.2 %copy-start.7 = (f32[384]{0:T(512)S(1)}, f32[384]{0:T(512)}, u32[]{:S(2)}) copy-start(f32[384]{0:T(512)} %param.13) | copy-start | bytes 4612
  8.0 78.0 %reduce-scatter.5.cloned.1.call-start = ((), (), s32[]{:S(2)}) async-start(), calls=%async_computation.2 | async-start | bytes 5898240 | tf_op jit(solution)/shard_map/reduce_scatter | solution.py:158
  9.0 10.3 %collective-permute-start.1 = (bf16[1,3,16,384]{3,2,1,0:T(8,128)(2,1)S(1)}, bf16[1,3,16,384]{3,2,1,0:T(8,128)(2,1)S(1)}, u32[]{:S(2)}, u32[]{:S(2)}) collective-permute-start(bf16[1,3,16,384]{3,2,1,0:T(8,128)(2,1)S(1)} %get-tuple-element.128), channel_id=1, source_target_pairs={{8,0},{16,8},{24,16},{9,1},{17,9},{25,17},{10,2},{18,10},{26,18},{... | collective-permute-start | bytes 110600 | tf_op jit(solution)/shard_map/ppermute | solution.py:21
  10.2 8.0 %collective-permute-start = (bf16[1,3,16,384]{3,2,1,0:T(8,128)(2,1)S(1)}, bf16[1,3,16,384]{3,2,1,0:T(8,128)(2,1)S(1)}, u32[]{:S(2)}, u32[]{:S(2)}) collective-permute-start(bf16[1,3,16,384]{3,2,1,0:T(8,128)(2,1)S(1)} %get-tuple-element.129), channel_id=1, source_target_pairs={{0,8},{8,16},{16,24},{1,9},{9,17},{17,25},{2,10},{10,18},{18,26},{... | collective-permute-start | bytes 110600 | tf_op jit(solution)/shard_map/ppermute | solution.py:19
  19.3 6.1 %collective-permute-start.2 = (bf16[1,14,3,384]{3,2,1,0:T(4,128)(2,1)S(1)}, bf16[1,14,3,384]{3,2,1,0:T(4,128)(2,1)S(1)}, u32[]{:S(2)}, u32[]{:S(2)}) collective-permute-start(bf16[1,14,3,384]{3,2,1,0:T(4,128)(2,1)S(1)} %get-tuple-element.125), channel_id=1, source_target_pairs={{0,4},{1,5},{2,6},{3,7},{8,12},{9,13},{10,14},{11,15},{16,20},{17,... | collective-permute-start | bytes 96776 | tf_op jit(solution)/shard_map/ppermute | solution.py:19
  23.1 5.9 %collective-permute-start.3 = (bf16[1,14,3,384]{3,2,1,0:T(4,128)(2,1)S(1)}, bf16[1,14,3,384]{3,2,1,0:T(4,128)(2,1)S(1)}, u32[]{:S(2)}, u32[]{:S(2)}) collective-permute-start(bf16[1,14,3,384]{3,2,1,0:T(4,128)(2,1)S(1)} %get-tuple-element.126), channel_id=1, source_target_pairs={{4,0},{5,1},{6,2},{7,3},{12,8},{13,9},{14,10},{15,11},{20,16},{21,... | collective-permute-start | bytes 96776 | tf_op jit(solution)/shard_map/ppermute | solution.py:21
  29.2 2.0 copy-start.4
  29.2 2.0 copy-start.8
  29.2 2.1 %copy-start.5 = (f32[1536]{0:T(1024)S(1)}, f32[1536]{0:T(1024)}, u32[]{:S(2)}) copy-start(f32[1536]{0:T(1024)} %param.17) | copy-start | bytes 18436
  31.3 1.3 copy-start.1
  31.4 1.3 copy-start.2
  31.4 1.3 copy-start.6
  31.4 1.2 copy-start.9
  37.7 149.1 %all-reduce.3.cloned.1.call-start = ((), (), s32[]{:S(2)}) async-start(), calls=%async_computation.3 | async-start | bytes 172032 | tf_op jit(solution)/shard_map/psum | solution.py:160
  40.5 0.6 copy-start.3
  41.2 149.2 %reduce-scatter.7.cloned.1.call-start = ((), (), s32[]{:S(2)}) async-start(), calls=%async_computation.4 | async-start | bytes 1769472
  90.7 47.2 %collective-permute-start.5 = (f32[3,16,384]{2,1,0:T(8,128)S(1)}, f32[3,16,384]{2,1,0:T(8,128)S(1)}, u32[]{:S(2)}, u32[]{:S(2)}) collective-permute-start(f32[3,16,384]{2,1,0:T(8,128)S(1)} %bitcast.132), channel_id=1, source_target_pairs={{8,0},{16,8},{24,16},{9,1},{17,9},{25,17},{10,2},{18,10},{26,18},{... | collective-permute-start | bytes 221192 | tf_op jit(solution)/shard_map/ppermute | solution.py:21
  92.0 45.9 %collective-permute-start.4 = (f32[3,16,384]{2,1,0:T(8,128)S(1)}, f32[3,16,384]{2,1,0:T(8,128)S(1)}, u32[]{:S(2)}, u32[]{:S(2)}) collective-permute-start(f32[3,16,384]{2,1,0:T(8,128)S(1)} %bitcast.131), channel_id=1, source_target_pairs={{0,8},{8,16},{16,24},{1,9},{9,17},{17,25},{2,10},{10,18},{18,26},{... | collective-permute-start | bytes 221192 | tf_op jit(solution)/shard_map/ppermute | solution.py:19
  137.9 50.4 %collective-permute-start.6 = (f32[14,3,384]{2,1,0:T(4,128)S(1)}, f32[14,3,384]{2,1,0:T(4,128)S(1)}, u32[]{:S(2)}, u32[]{:S(2)}) collective-permute-start(f32[14,3,384]{2,1,0:T(4,128)S(1)} %get-tuple-element.117), channel_id=1, source_target_pairs={{4,0},{5,1},{6,2},{7,3},{12,8},{13,9},{14,10},{15,11},{20,16},{21,... | collective-permute-start | bytes 193544 | tf_op jit(solution)/shard_map/ppermute | solution.py:21
  139.2 49.1 %collective-permute-start.7 = (f32[14,3,384]{2,1,0:T(4,128)S(1)}, f32[14,3,384]{2,1,0:T(4,128)S(1)}, u32[]{:S(2)}, u32[]{:S(2)}) collective-permute-start(f32[14,3,384]{2,1,0:T(4,128)S(1)} %get-tuple-element.118), channel_id=1, source_target_pairs={{0,4},{1,5},{2,6},{3,7},{8,12},{9,13},{10,14},{11,15},{16,20},{17,... | collective-permute-start | bytes 193544 | tf_op jit(solution)/shard_map/ppermute | solution.py:19
Sparse Core Ops, SparseCore 0:
  37.8 48.1 reduce-scatter.4
  90.7 65.2 reduce-scatter.6
Sparse Core Ops, SparseCore 1:
  44.3 142.4 all-reduce.2
where the time goes:
time: 202 us; the launch traced here: 200 us
  waiting for transfers between devices  91.5 us (45%)
  blocking collectives  40.1 us (20%)
  starting transfers between devices  23.8 us (12%)
  between operations  16.3 us (8%)
  local copies, waits for them, and re-layouts  13.4 us (7%)
  other arithmetic  11.3 us (6%)
  matrix products  3.6 us (2%)
    reduce_scatter x1, waiting for transfers between devices, per_device(): lax.psum_scatter(stacked, 'rep', scatter_dimension=1, tiled=True)  44.8 us
    psum x1, waiting for transfers between devices, per_device(): lax.psum((gker, vectors, gbexp), ('rows', 'cols', 'rep'))  43 us
    psum x1, blocking collectives, per_device(): lax.psum((gker, vectors, gbexp), ('rows', 'cols', 'rep'))  40.1 us
    ppermute x4, starting transfers between devices, extended(): lax.ppermute(tail, axis, [(i, (i + 1) % count) for i in range(ends)])  18.5 us
    unnamed x33, local copies, waits for them, and re-layouts  8.26 us
    ppermute x4, starting transfers between devices, extended(): lax.ppermute(head, axis, [((i + 1) % count, i) for i in range(ends)])  5.16 us
  transfers between devices with their start and end apart: 11, of which 3 were waited for; matrix products, arithmetic and copies ran while one was open for 8% of the time, Pallas kernels for 0%

commit v1 on v0

--- a/solution.py
+++ b/solution.py
@@ -1,7 +1,19 @@
+import functools
+
 import jax
 import jax.numpy as jnp
 from jax import lax
+from jax.experimental import pallas as pl
+from jax.experimental.pallas import tpu as pltpu
 from jax.sharding import PartitionSpec as P
+
+MESH = pl.DeviceIdType.MESH
+F32, BF16 = jnp.float32, jnp.bfloat16
+LANES = 128
+PIECE = 16
+ORDERS = ("yxz", "xyz", "zyx", "xyz", "yxz", "xyz")
+DIRECTIONS = ((-1, 0), (1, 0), (0, -1), (0, 1), (-1, -1), (-1, 1), (1, -1), (1, 1))
+SIZES = {"y": 2, "x": 2, "z": 4}
 
 EPS = 1e-06
 INV_ROOT_TWO = 0.7071067811865476
@@ -171,6 +183,567 @@
     )
 
 
+def pack_rows(value):
+    half = value.shape[0] // 2
+    return jnp.concatenate([value[:half, :8], value[half:, :8]], axis=1)
+
+
+def halo_source(cells, dz, dx):
+    rows = cells
+    if dz == -1:
+        rows = cells[:4] if dx else cells[:3]
+    elif dz == 1:
+        rows = cells[4:] if dx else cells[5:]
+    if dx == 0:
+        return rows.astype(BF16)
+    return pack_rows(rows[:, :8] if dx == -1 else rows[:, 8:]).astype(BF16)
+
+
+def halo_target(padded, landed, dz, dx):
+    if dx:
+        half = landed.shape[0]
+        landed = jnp.concatenate([landed[:, :8], landed[:, 8:]], axis=0)
+        if dz == 1:
+            landed = landed[1:]
+        elif dz == -1:
+            landed = landed[:3]
+    rows = slice(3, 11) if dz == 0 else (slice(0, 3) if dz == 1 else slice(11, 14))
+    columns = slice(8, 24) if dx == 0 else (slice(0, 8) if dx == 1 else slice(24, 32))
+    padded[rows, columns, :] = landed
+
+
+def halo_shape(dz, dx, chans):
+    if dx == 0:
+        return (3, 16, chans)
+    return (4 if dz == 0 else 2, 16, chans)
+
+
+def fused_kernel(
+    sizes,
+    scale,
+    x_ref,
+    gout_ref,
+    dwk_ref,
+    dwb_ref,
+    gain_ref,
+    lnb_ref,
+    wexp_hbm,
+    bexp_ref,
+    wred_hbm,
+    bred_ref,
+    ls_ref,
+    out_ref,
+    gin_ref,
+    gexp_ref,
+    gred_ref,
+    gker_ref,
+    gvec_ref,
+    gbexp_ref,
+    wexp,
+    wred,
+    xp,
+    gp,
+    work,
+    xhat_s,
+    lhs_t,
+    main0,
+    main1,
+    rem,
+    grad_out_blocks,
+    landed0,
+    xsend,
+    xland,
+    gsend,
+    gland,
+    small,
+    small_send,
+    small_land,
+    zsend,
+    zland,
+    final,
+    keeps,
+    sends,
+    lands,
+    wsem,
+    halo_sems,
+    core_sems,
+    part_sems,
+    small_sems,
+):
+    zn, xn, rn = sizes
+    z, x, r = lax.axis_index("rows"), lax.axis_index("cols"), lax.axis_index("rep")
+    y, c = r // 2, r % 2
+    chans = x_ref.shape[-1]
+    hidden = wexp.shape[1]
+    core_mate = {"rows": z, "cols": x, "rep": 2 * y + 1 - c}
+    y_mate = {"rows": z, "cols": x, "rep": 2 * (1 - y) + c}
+    x_mate = {"rows": z, "cols": 1 - x, "rep": r}
+
+    def z_mate(d):
+        return {"rows": (z + d) % zn, "cols": x, "rep": r}
+
+    weights = [
+        pltpu.make_async_copy(wexp_hbm, wexp, wsem.at[0]),
+        pltpu.make_async_copy(wred_hbm, wred, wsem.at[1]),
+    ]
+    for copy in weights:
+        copy.start()
+
+    def inside(a, b):
+        return (a >= 0) & (a < zn) & (b >= 0) & (b < xn)
+
+    barrier = pltpu.get_barrier_semaphore()
+    greeted = jnp.int32(6)
+    for mate in [core_mate, y_mate, x_mate] + [z_mate(d) for d in (1, 2, 3)]:
+        pl.semaphore_signal(barrier, inc=1, device_id=mate, device_id_type=MESH)
+    for dz, dx in DIRECTIONS:
+        if dx == 0 or dz == 0:
+            continue
+        near = inside(z + dz, x + dx)
+
+        @pl.when(near)
+        def _():
+            pl.semaphore_signal(
+                barrier,
+                inc=1,
+                device_id={"rows": z + dz, "cols": x + dx, "rep": r},
+                device_id_type=MESH,
+            )
+
+        greeted = greeted + near.astype(jnp.int32)
+
+    cells = x_ref[0].astype(F32)
+    for n, (dz, dx) in enumerate(DIRECTIONS):
+        xsend[n][...] = halo_source(cells, dz, dx)
+    xp[...] = jnp.zeros_like(xp)
+    gp[...] = jnp.zeros_like(gp)
+    xp[3:11, 8:24, :] = cells
+    pl.semaphore_wait(barrier, greeted)
+
+    def halo_copy(which, n):
+        source, target = ((xsend, xland), (gsend, gland))[which]
+        dz, dx = DIRECTIONS[n]
+        return pltpu.make_async_remote_copy(
+            src_ref=source[n],
+            dst_ref=target[n],
+            send_sem=halo_sems.at[which, 0, n],
+            recv_sem=halo_sems.at[which, 1, n],
+            device_id={"rows": z + dz, "cols": x + dx, "rep": r},
+            device_id_type=MESH,
+        )
+
+    def halo_start(which):
+        for n, (dz, dx) in enumerate(DIRECTIONS):
+            pl.when(inside(z + dz, x + dx))(lambda n=n: halo_copy(which, n).start())
+
+    def halo_finish(which, padded):
+        landed = (xland, gland)[which]
+        for n, (dz, dx) in enumerate(DIRECTIONS):
+
+            @pl.when(inside(z - dz, x - dx))
+            def _(n=n, dz=dz, dx=dx):
+                halo_copy(which, n).wait_recv()
+                halo_target(padded, landed[n][...].astype(F32), dz, dx)
+
+    def halo_sent(which):
+        for n, (dz, dx) in enumerate(DIRECTIONS):
+            pl.when(inside(z + dz, x + dx))(lambda n=n: halo_copy(which, n).wait_send())
+
+    halo_start(0)
+    grad = gout_ref[0].astype(F32).reshape(-1, chans)
+    scaled = grad * ls_ref[...]
+    g_branch = scaled.astype(BF16)
+    small[...] = jnp.zeros_like(small)
+    small[52:53, :] = jnp.sum(scaled, axis=0, keepdims=True)
+    weights[1].wait()
+    contract_last = (((1,), (1,)), ((), ()))
+    g_act = lax.dot_general(g_branch, wred[...], contract_last, preferred_element_type=F32)
+    lhs_t[1] = scaled.T.astype(BF16).reshape(rn, chans // rn, 128)
+    halo_finish(0, xp)
+
+    def conv_chunk(n, carry):
+        ch = pl.ds(pl.multiple_of(n * LANES, LANES), LANES)
+        total = jnp.zeros((8, 16, LANES), F32) + dwb_ref[:, ch]
+        for j in range(7):
+            shifted = xp[:, 5 + j : 21 + j, ch]
+            for i in range(7):
+                total = total + dwk_ref[7 * i + j : 7 * i + j + 1, ch] * shifted[i : i + 8]
+        work[:, ch] = total.reshape(128, LANES)
+        return carry
+
+    lax.fori_loop(0, chans // LANES, conv_chunk, 0)
+    conv = work[...]
+    centered = conv - jnp.mean(conv, axis=-1, keepdims=True)
+    rstd = lax.rsqrt(jnp.mean(centered * centered, axis=-1, keepdims=True) + EPS)
+    xhat = centered * rstd
+    xhat_s[...] = xhat
+    normed32 = xhat * gain_ref[...] + lnb_ref[...]
+    normed = normed32.astype(BF16)
+    lhs_t[0] = normed32.T.astype(BF16).reshape(rn, chans // rn, 128)
+    weights[0].wait()
+    pre = jnp.dot(normed, wexp[...], preferred_element_type=F32) + bexp_ref[...]
+    cdf = 0.5 * (1.0 + lax.erf(pre * INV_ROOT_TWO))
+    act32 = pre * cdf
+    act = act32.astype(BF16)
+    pdf = jnp.exp(-0.5 * pre * pre) * INV_ROOT_TWO_PI
+    g_pre = g_act * (cdf + pre * pdf)
+    bexp_sum = jnp.sum(g_pre, axis=0, keepdims=True)
+    for n in range(hidden // chans):
+        small[54 + n : 55 + n, :] = bexp_sum[:, n * chans : (n + 1) * chans]
+    g_pre_b = g_pre.astype(BF16)
+
+    low = lax.broadcasted_iota(jnp.int32, (128, LANES), 1) < LANES // 2
+    zero = jnp.zeros((128, LANES), F32)
+    for n in range(zn):
+        at = 3 * LANES * n
+        even, odd = slice(2 * n * LANES, (2 * n + 1) * LANES), slice((2 * n + 1) * LANES, (2 * n + 2) * LANES)
+        main0[:, even] = g_pre_b[:, at : at + LANES]
+        main0[:, odd] = g_pre_b[:, at + 2 * LANES : at + 3 * LANES]
+        main1[:, even] = act[:, at : at + LANES]
+        main1[:, odd] = act[:, at + 2 * LANES : at + 3 * LANES]
+        middle = g_pre[:, at + LANES : at + 2 * LANES]
+        rolled = pltpu.roll(act32[:, at + LANES : at + 2 * LANES], LANES // 2, 1)
+        rem[:128, even] = jnp.where(low, middle, zero).astype(BF16)
+        rem[128:, even] = jnp.where(low, zero, rolled).astype(BF16)
+        rem[:128, odd] = jnp.where(low, zero, middle).astype(BF16)
+        rem[128:, odd] = jnp.where(low, rolled, zero).astype(BF16)
+
+    def products(owner):
+        left0 = jnp.concatenate([lhs_t[0, owner], lhs_t[0, 2 + owner]], axis=0)
+        left1 = jnp.concatenate([lhs_t[1, owner], lhs_t[1, 2 + owner]], axis=0)
+        both = jnp.concatenate([left0, left1], axis=1)
+        rows = chans // rn
+        for k, (left, right) in enumerate(((left0, main0), (left1, main1), (both, rem))):
+            for zz in range(zn):
+                block = jnp.dot(
+                    left, right[:, 2 * zz * LANES : (2 * zz + 2) * LANES], preferred_element_type=F32
+                ).astype(BF16)
+                for xx in range(xn):
+                    for yy in range(2):
+                        part = block[yy * rows : (yy + 1) * rows, xx * LANES : (xx + 1) * LANES]
+                        grad_out_blocks[owner, :, yy, xx, zz, k] = part.reshape(-1, PIECE, LANES)
+
+    def core_copy(p):
+        return pltpu.make_async_remote_copy(
+            src_ref=grad_out_blocks.at[1 - c, p],
+            dst_ref=landed0.at[p],
+            send_sem=core_sems.at[0, p],
+            recv_sem=core_sems.at[1, p],
+            device_id=core_mate,
+            device_id_type=MESH,
+        )
+
+    parts = len(ORDERS)
+    products(1 - c)
+    for p in range(parts):
+        core_copy(p).start()
+    products(c)
+
+    def place(dims, axis, index):
+        return tuple(index if d == axis else slice(None) for d in dims)
+
+    def stage_copies(p, s):
+        axis = ORDERS[p][s]
+        if axis == "z":
+            return [
+                pltpu.make_async_remote_copy(
+                    src_ref=sends[p][s].at[d - 1],
+                    dst_ref=lands[p][s].at[d - 1],
+                    send_sem=part_sems.at[p, s, 0, d - 1],
+                    recv_sem=part_sems.at[p, s, 1, d - 1],
+                    device_id=z_mate(d),
+                    device_id_type=MESH,
+                )
+                for d in (1, 2, 3)
+            ]
+        return [
+            pltpu.make_async_remote_copy(
+                src_ref=sends[p][s].at[0],
+                dst_ref=lands[p][s].at[0],
+                send_sem=part_sems.at[p, s, 0, 0],
+                recv_sem=part_sems.at[p, s, 1, 0],
+                device_id=y_mate if axis == "y" else x_mate,
+                device_id_type=MESH,
+            )
+        ]
+
+    def load(p, s, at):
+        if s == 0:
+            return grad_out_blocks[(c, p) + at].astype(F32) + landed0[(p,) + at].astype(F32)
+        total = keeps[p][s - 1][at]
+        for d in range(lands[p][s - 1].shape[0]):
+            total = total + lands[p][s - 1][(d,) + at].astype(F32)
+        return total
+
+    def stage(p, s):
+        if s == 0:
+            core_copy(p).wait_recv()
+        else:
+            for copy in stage_copies(p, s - 1):
+                copy.wait_recv()
+        dims = [d for d in "yxz" if d not in ORDERS[p][:s]]
+        if s == 3:
+            final[:, p * PIECE : (p + 1) * PIECE, :] = load(p, s, ())
+            return
+        axis = ORDERS[p][s]
+        copies = stage_copies(p, s)
+        if axis == "z":
+            for d in (1, 2, 3):
+                sends[p][s][d - 1] = load(p, s, place(dims, "z", (z + d) % zn)).astype(BF16)
+                copies[d - 1].start()
+            keeps[p][s][...] = load(p, s, place(dims, "z", z))
+        else:
+            mine = y if axis == "y" else x
+            sends[p][s][0] = load(p, s, place(dims, axis, 1 - mine)).astype(BF16)
+            copies[0].start()
+            keeps[p][s][...] = load(p, s, place(dims, axis, mine))
+
+    for p in range(parts):
+        stage(p, 0)
+
+    g_normed = lax.dot_general(g_pre_b, wexp[...], contract_last, preferred_element_type=F32)
+    xhat = xhat_s[...]
+    small[50:51, :] = jnp.sum(g_normed * xhat, axis=0, keepdims=True)
+    small[51:52, :] = jnp.sum(g_normed, axis=0, keepdims=True)
+    gx = g_normed * gain_ref[...]
+    g_conv = rstd * (
+        gx
+        - jnp.mean(gx, axis=-1, keepdims=True)
+        - xhat * jnp.mean(gx * xhat, axis=-1, keepdims=True)
+    )
+    small[49:50, :] = jnp.sum(g_conv, axis=0, keepdims=True)
+    g_cells = g_conv.reshape(8, 16, chans)
+    for n, (dz, dx) in enumerate(DIRECTIONS):
+        gsend[n][...] = halo_source(g_cells, dz, dx)
+    halo_start(1)
+    gp[3:11, 8:24, :] = g_cells
+
+    branch = jnp.dot(act, wred[...], preferred_element_type=F32) + bred_ref[...]
+    small[53:54, :] = jnp.sum(grad * branch, axis=0, keepdims=True)
+    inner = x_ref[0].astype(F32).reshape(-1, chans)
+    out_ref[0] = (inner + ls_ref[...] * branch).astype(BF16).reshape(8, 16, chans)
+
+    def kernel_chunk(n, carry):
+        ch = pl.ds(pl.multiple_of(n * LANES, LANES), LANES)
+        own = gp[3:11, 8:24, ch]
+        for j in range(7):
+            shifted = xp[:, 5 + j : 21 + j, ch]
+            for i in range(7):
+                terms = jnp.sum((own * shifted[i : i + 8]).reshape(16, 8, LANES), axis=0)
+                small[7 * i + j : 7 * i + j + 1, ch] = jnp.sum(terms, axis=0, keepdims=True)
+        return carry
+
+    lax.fori_loop(0, chans // LANES, kernel_chunk, 0)
+
+    half = small.shape[0] // 2
+
+    def small_copy(n, source, target, mate):
+        return pltpu.make_async_remote_copy(
+            src_ref=source,
+            dst_ref=target,
+            send_sem=small_sems.at[0, n],
+            recv_sem=small_sems.at[1, n],
+            device_id=mate,
+            device_id_type=MESH,
+        )
+
+    moves = [small_copy(n, small_send.at[n], small_land.at[n], m) for n, m in enumerate((core_mate, y_mate, x_mate))]
+    z_moves = [small_copy(2 + d, zsend, zland.at[d - 1], z_mate(d)) for d in (1, 2, 3)]
+    other_rows = pl.ds(pl.multiple_of((1 - c) * half, half), half)
+    my_rows = pl.ds(pl.multiple_of(c * half, half), half)
+    small_send[0] = small[other_rows, :]
+    moves[0].start()
+
+    for p in range(parts):
+        stage(p, 1)
+
+    moves[0].wait_recv()
+    small_send[1] = small[my_rows, :] + small_land[0]
+    moves[1].start()
+
+    halo_finish(1, gp)
+
+    def input_chunk(n, carry):
+        ch = pl.ds(pl.multiple_of(n * LANES, LANES), LANES)
+        total = gout_ref[0, :, :, ch].astype(F32)
+        for j in range(7):
+            shifted = gp[:, 11 - j : 27 - j, ch]
+            for i in range(7):
+                total = total + dwk_ref[7 * i + j : 7 * i + j + 1, ch] * shifted[6 - i : 14 - i]
+        gin_ref[0, :, :, ch] = total.astype(BF16)
+        return carry
+
+    moves[1].wait_recv()
+    small_send[2] = small_send[1] + small_land[1]
+    moves[2].start()
+    lax.fori_loop(0, chans // LANES, input_chunk, 0)
+
+    moves[2].wait_recv()
+    zsend[...] = (small_send[2] + small_land[2]).astype(BF16)
+    for move in z_moves:
+        move.start()
+
+    for p in range(parts):
+        stage(p, 2)
+
+    for move in z_moves:
+        move.wait_recv()
+    quarter = [zsend[...].astype(F32)] + [zland[d].astype(F32) for d in range(3)]
+    total = jnp.zeros_like(quarter[0])
+    for at in range(zn):
+        d = (z - at) % zn
+        term = quarter[0]
+        for k in (1, 2, 3):
+            term = jnp.where(d == k, quarter[k], term)
+        total = total + term
+    small_send[3] = total * scale
+    last = small_copy(6, small_send.at[3], small_land.at[3], core_mate)
+    last.start()
+
+    for p in range(parts):
+        stage(p, 3)
+    blocks = final[...] * scale
+    wide = LANES + LANES // 2
+    m0, m1, mixed = blocks[0], blocks[1], blocks[2]
+    first, second = mixed[:, : LANES // 2], mixed[:, LANES // 2 :]
+
+    @pl.when(x == 0)
+    def _():
+        gexp_ref[:, :LANES] = m0
+        gexp_ref[:, LANES:wide] = first
+        gred_ref[:, :LANES] = m1
+        gred_ref[:, LANES:wide] = second
+
+    @pl.when(x == 1)
+    def _():
+        gexp_ref[...] = jnp.concatenate([second, m0], axis=1)
+        gred_ref[...] = jnp.concatenate([first, m1], axis=1)
+
+    last.wait_recv()
+    small[my_rows, :] = small_send[3]
+    small[other_rows, :] = small_land[3]
+    for i in range(7):
+        gker_ref[i] = small[7 * i : 7 * i + 7, :]
+    gvec_ref[...] = small[49:54, :]
+    for n in range(hidden // chans):
+        gbexp_ref[:, n * chans : (n + 1) * chans] = small[54 + n : 55 + n, :]
+
+    halo_sent(0)
+    halo_sent(1)
+    for p in range(parts):
+        core_copy(p).wait_send()
+        for s in range(3):
+            for copy in stage_copies(p, s):
+                copy.wait_send()
+    for move in moves + z_moves + [last]:
+        move.wait_send()
+
+
+def fused(mesh_sizes, *args):
+    (
+        feature_map,
+        dw_kernel,
+        dw_bias,
+        layer_norm_gain,
+        layer_norm_bias,
+        w_expand,
+        b_expand,
+        w_reduce,
+        b_reduce,
+        layer_scale,
+        cotangent,
+    ) = args
+    zn, xn, rn = mesh_sizes
+    _, height, width, chans = feature_map.shape
+    hidden = w_expand.shape[1]
+    pixels = height * width * zn * xn * rn
+    scale = float(pixels) ** -0.5
+    vmem = pl.BlockSpec(memory_space=pltpu.VMEM)
+    anywhere = pl.BlockSpec(memory_space=pl.ANY)
+    parts = len(ORDERS)
+    block = (3, PIECE, LANES)
+    keeps, sends, lands = [], [], []
+    for order in ORDERS:
+        keeps.append([])
+        sends.append([])
+        lands.append([])
+        for s in range(3):
+            left = tuple(SIZES[d] for d in "yxz" if d not in order[: s + 1])
+            copies = 3 if order[s] == "z" else 1
+            keeps[-1].append(pltpu.VMEM(left + block, F32))
+            sends[-1].append(pltpu.VMEM((copies,) + left + block, BF16))
+            lands[-1].append(pltpu.VMEM((copies,) + left + block, BF16))
+    halos = [pltpu.VMEM(halo_shape(dz, dx, chans), BF16) for dz, dx in DIRECTIONS]
+    scratch = dict(
+        wexp=pltpu.VMEM(w_expand.shape, BF16),
+        wred=pltpu.VMEM(w_reduce.shape, BF16),
+        xp=pltpu.VMEM((14, 32, chans), F32),
+        gp=pltpu.VMEM((14, 32, chans), F32),
+        work=pltpu.VMEM((128, chans), F32),
+        xhat_s=pltpu.VMEM((128, chans), F32),
+        lhs_t=pltpu.VMEM((2, rn, chans // rn, 128), BF16),
+        main0=pltpu.VMEM((128, 2 * zn * LANES), BF16),
+        main1=pltpu.VMEM((128, 2 * zn * LANES), BF16),
+        rem=pltpu.VMEM((256, 2 * zn * LANES), BF16),
+        grad_out_blocks=pltpu.VMEM((2, parts, 2, xn, zn) + block, BF16),
+        landed0=pltpu.VMEM((parts, 2, xn, zn) + block, BF16),
+        xsend=list(halos),
+        xland=list(halos),
+        gsend=list(halos),
+        gland=list(halos),
+        small=pltpu.VMEM((64, chans), F32),
+        small_send=pltpu.VMEM((4, 32, chans), F32),
+        small_land=pltpu.VMEM((4, 32, chans), F32),
+        zsend=pltpu.VMEM((32, chans), BF16),
+        zland=pltpu.VMEM((3, 32, chans), BF16),
+        final=pltpu.VMEM((3, parts * PIECE, LANES), F32),
+        keeps=keeps,
+        sends=sends,
+        lands=lands,
+        wsem=pltpu.SemaphoreType.DMA((2,)),
+        halo_sems=pltpu.SemaphoreType.DMA((2, 2, 8)),
+        core_sems=pltpu.SemaphoreType.DMA((2, parts)),
+        part_sems=pltpu.SemaphoreType.DMA((parts, 3, 2, 3)),
+        small_sems=pltpu.SemaphoreType.DMA((2, 7)),
+    )
+    rows, columns = chans // rn, hidden // (zn * xn)
+    outs = pl.pallas_call(
+        functools.partial(fused_kernel, mesh_sizes, scale),
+        out_shape=[
+            jax.ShapeDtypeStruct(feature_map.shape, BF16),
+            jax.ShapeDtypeStruct(feature_map.shape, BF16),
+            jax.ShapeDtypeStruct((rows, columns), F32),
+            jax.ShapeDtypeStruct((rows, columns), F32),
+            jax.ShapeDtypeStruct(dw_kernel.shape, F32),
+            jax.ShapeDtypeStruct((5, chans), F32),
+            jax.ShapeDtypeStruct((1, hidden), F32),
+        ],
+        in_specs=[vmem] * 6 + [anywhere, vmem, anywhere, vmem, vmem],
+        out_specs=[vmem] * 7,
+        scratch_shapes=list(scratch.values()),
+        compiler_params=pltpu.CompilerParams(
+            collective_id=0, has_side_effects=True, vmem_limit_bytes=48 * 1024 * 1024
+        ),
+    )(
+        feature_map,
+        cotangent,
+        dw_kernel.reshape(49, chans),
+        dw_bias.reshape(1, -1),
+        layer_norm_gain.reshape(1, -1),
+        layer_norm_bias.reshape(1, -1),
+        w_expand,
+        b_expand.reshape(1, -1),
+        w_reduce,
+        b_reduce.reshape(1, -1),
+        layer_scale.reshape(1, -1),
+    )
+    return tuple(outs[:6]) + (outs[6].reshape(-1),)
+
+
+def fits(sizes):
+    return sizes == (4, 2, 4)
+
+
 def solution(mesh):
     in_specs = (
         P("rep", "rows", "cols", None),
@@ -194,6 +767,8 @@
         P(),
         P(),
     )
+    sizes = tuple(mesh.shape[a] for a in ("rows", "cols", "rep"))
+    body = functools.partial(fused, sizes) if fits(sizes) else per_device
     return jax.shard_map(
-        per_device, mesh=mesh, in_specs=in_specs, out_specs=out_specs, check_vma=False
-    )
+        body, mesh=mesh, in_specs=in_specs, out_specs=out_specs, check_vma=False
+    )

time: 202 us -> 55.5 us (0.27)
  waiting for transfers between devices: 91.5 us -> 0 us
  Pallas kernels: 0 us -> 40.6 us
  blocking collectives: 40.1 us -> 0 us
  starting transfers between devices: 23.8 us -> 0 us
  between operations: 16.3 us -> 0.66 us
  other arithmetic: 11.3 us -> 0.62 us
  matrix products: 3.6 us -> 0 us
    reduce_scatter x1 -> x0, waiting for transfers between devices: 44.8 us -> none  [per_device(): lax.psum_scatter(stacked, 'rep', scatter_dimension=1, tiled=True)]
    psum x1 -> x0, waiting for transfers between devices: 43 us -> none  [per_device(): lax.psum((gker, vectors, gbexp), ('rows', 'cols', 'rep'))]
    pallas_call x0 -> x1, Pallas kernels: none -> 40.6 us  [fused(): pl.pallas_call(functools.partial(fused_kernel, mesh_sizes, scale), out_sh...]
    psum x1 -> x0, blocking collectives: 40.1 us -> none  [per_device(): lax.psum((gker, vectors, gbexp), ('rows', 'cols', 'rep'))]
    ppermute x8 -> x0, starting transfers between devices: 23.7 us -> none  [the longest x4 18.5 us: extended(): lax.ppermute(tail, axis, [(i, (i + 1) % count) for i in range(ends)])]
    reshape x0 -> x7, local copies, waits for them, and re-layouts: none -> 5.02 us  [the longest x1 0.9 us: fused(): dw_kernel.reshape(49, chans)]
    slice x7 -> x0, local copies, waits for them, and re-layouts: 4.51 us -> none  [the longest x3 3.42 us: depthwise(): kernel[i, j] * padded[i:i + height, j:j + width].astype(jnp.float32)]
    ppermute x8 -> x0, waiting for transfers between devices: 3.66 us -> none  [the longest x4 3.65 us: extended(): lax.ppermute(head, axis, [((i + 1) % count, i) for i in range(ends)])]
  transfers between devices with their start and end apart: 11 -> 0, of which waited for: 3 -> 0; matrix products, arithmetic and copies ran while one was open for 8% -> 0% of each run, Pallas kernels for 0% -> 0%
where the time goes in v1:
time: 55.5 us; the launch traced here: 55 us
  Pallas kernels  40.6 us (73%)
  local copies, waits for them, and re-layouts  13.1 us (24%)
  between operations  0.66 us (1%)
  other arithmetic  0.62 us (1%)
    pallas_call x1, Pallas kernels, fused(): pl.pallas_call(functools.partial(fused_kernel, mesh_sizes, scale), out_sh...  40.6 us
    unnamed x14, local copies, waits for them, and re-layouts  8.12 us

profile of v1, /device:TPU:0, one launch (start us, length us, event | category | flops | bytes accessed | tf_op | source)
XLA Modules:
  0.0 55.0 jit_solution(3626076819660126103)
XLA Ops:
  0.6 0.9 %reshape.38.dwk_ref = f32[49,384]{1,0:T(8,128)S(1)} reshape(f32[7,7,384]{2,1,0:T(8,128)} %param.12) | data formatting | bytes 150528 | tf_op jit(solution)/shard_map/reshape | solution.py:730
  1.5 0.7 %reshape.42.bexp_ref = f32[1,1536]{1,0:T(1,128)S(1)} reshape(f32[1536]{0:T(1024)} %param.17) | data formatting | bytes 12288 | tf_op jit(solution)/shard_map/reshape | solution.py:735
  2.2 0.7 %reshape.39.dwb_ref = f32[1,384]{1,0:T(1,128)S(1)} reshape(f32[384]{0:T(512)} %param.13) | data formatting | bytes 3072 | tf_op jit(solution)/shard_map/reshape | solution.py:731
  2.9 0.7 %reshape.40.gain_ref = f32[1,384]{1,0:T(1,128)S(1)} reshape(f32[384]{0:T(512)} %param.14) | data formatting | bytes 3072 | tf_op jit(solution)/shard_map/reshape | solution.py:732
  3.6 0.7 %reshape.41.lnb_ref = f32[1,384]{1,0:T(1,128)S(1)} reshape(f32[384]{0:T(512)} %param.15) | data formatting | bytes 3072 | tf_op jit(solution)/shard_map/reshape | solution.py:733
  4.3 0.7 %reshape.43.bred_ref = f32[1,384]{1,0:T(1,128)S(1)} reshape(f32[384]{0:T(512)} %param.19) | data formatting | bytes 3072 | tf_op jit(solution)/shard_map/reshape | solution.py:737
  5.0 0.7 %reshape.44.ls_ref = f32[1,384]{1,0:T(1,128)S(1)} reshape(f32[384]{0:T(512)} %param.20) | data formatting | bytes 3072 | tf_op jit(solution)/shard_map/reshape | solution.py:738
  5.7 0.0 copy-start
  5.7 1.3 %copy-done = bf16[384,1536]{1,0:T(8,128)(2,1)S(1)} copy-done((bf16[384,1536]{1,0:T(8,128)(2,1)S(1)}, bf16[384,1536]{1,0:T(8,128)(2,1)}, u32[]{:S(2)}) %copy-start) | copy-done | bytes 1179672
  6.9 0.0 copy-start.1
  6.9 1.3 %copy-done.1 = bf16[1536,384]{1,0:T(8,128)(2,1)S(1)} copy-done((bf16[1536,384]{1,0:T(8,128)(2,1)S(1)}, bf16[1536,384]{1,0:T(8,128)(2,1)}, u32[]{:S(2)}) %copy-start.1) | copy-done | bytes 1179672
  8.2 0.0 copy-start.2
  8.2 0.9 %copy-done.2 = bf16[1,8,16,384]{3,2,1,0:T(8,128)(2,1)S(1)} copy-done((bf16[1,8,16,384]{3,2,1,0:T(8,128)(2,1)S(1)}, bf16[1,8,16,384]{3,2,1,0:T(8,128)(2,1)}, u32[]{:S(2)}) %copy-start.2) | copy-done | bytes 98328
  9.1 0.0 copy-start.3
  9.1 0.9 %copy-done.3 = bf16[1,8,16,384]{3,2,1,0:T(8,128)(2,1)S(1)} copy-done((bf16[1,8,16,384]{3,2,1,0:T(8,128)(2,1)S(1)}, bf16[1,8,16,384]{3,2,1,0:T(8,128)(2,1)}, u32[]{:S(2)}) %copy-start.3) | copy-done | bytes 98328
  10.0 40.6 %shard_map.162 = (bf16[1,8,16,384]{3,2,1,0:T(8,128)(2,1)S(1)}, bf16[1,8,16,384]{3,2,1,0:T(8,128)(2,1)S(1)}, f32[96,192]{1,0:T(8,128)S(1)}, f32[96,192]{1,0:T(8,1...) custom-call(bf16[1,8,16,384]{3,2,1,0:T(8,128)(2,1)S(1)} %copy-done.2, ...), custom_call_target="tpu_custom_call" | custom-call | tf_op jit(solution)/shard_map/pallas_call | solution.py:710
  50.6 0.6 %reduce = f32[1536]{0:T(1024)} reduce(f32[1,1536]{1,0:T(1,128)S(1)} %get-tuple-element.20, f32[]{:T(128)} %constant.2), dimensions={0}, to_apply=%get-tuple-element.20.reduce_sub_computation | reduce | bytes 12292 | tf_op jit(solution)/shard_map/pallas_call | solution.py:710
  51.2 0.6 %copy.24 = bf16[1,8,16,384]{3,2,1,0:T(8,128)(2,1)} copy(bf16[1,8,16,384]{3,2,1,0:T(8,128)(2,1)S(1)} %get-tuple-element.28) | data formatting | bytes 196608
  51.9 0.6 %copy.25 = bf16[1,8,16,384]{3,2,1,0:T(8,128)(2,1)} copy(bf16[1,8,16,384]{3,2,1,0:T(8,128)(2,1)S(1)} %get-tuple-element.29) | data formatting | bytes 196608
  52.5 0.6 %copy.26 = f32[96,192]{1,0:T(8,128)} copy(f32[96,192]{1,0:T(8,128)S(1)} %get-tuple-element.30) | data formatting | bytes 147456
  53.2 0.6 %copy.27 = f32[96,192]{1,0:T(8,128)} copy(f32[96,192]{1,0:T(8,128)S(1)} %get-tuple-element.31) | data formatting | bytes 147456
  53.8 0.6 %copy.28 = f32[7,7,384]{2,1,0:T(8,128)} copy(f32[7,7,384]{2,1,0:T(8,128)S(1)} %get-tuple-element.32) | data formatting | bytes 150528
  54.4 0.6 %copy.29 = f32[5,384]{1,0:T(8,128)} copy(f32[5,384]{1,0:T(8,128)S(1)} %get-tuple-element.33) | data formatting | bytes 15360
Async XLA Ops:
  5.7 1.3 %copy-start = (bf16[384,1536]{1,0:T(8,128)(2,1)S(1)}, bf16[384,1536]{1,0:T(8,128)(2,1)}, u32[]{:S(2)}) copy-start(bf16[384,1536]{1,0:T(8,128)(2,1)} %wexp_hbm.1) | copy-start | bytes 3538948
  6.9 1.3 %copy-start.1 = (bf16[1536,384]{1,0:T(8,128)(2,1)S(1)}, bf16[1536,384]{1,0:T(8,128)(2,1)}, u32[]{:S(2)}) copy-start(bf16[1536,384]{1,0:T(8,128)(2,1)} %wred_hbm.1) | copy-start | bytes 3538948
  8.2 0.9 %copy-start.2 = (bf16[1,8,16,384]{3,2,1,0:T(8,128)(2,1)S(1)}, bf16[1,8,16,384]{3,2,1,0:T(8,128)(2,1)}, u32[]{:S(2)}) copy-start(bf16[1,8,16,384]{3,2,1,0:T(8,128)(2,1)} %x_ref.1) | copy-start | bytes 294916
  9.1 0.9 %copy-start.3 = (bf16[1,8,16,384]{3,2,1,0:T(8,128)(2,1)S(1)}, bf16[1,8,16,384]{3,2,1,0:T(8,128)(2,1)}, u32[]{:S(2)}) copy-start(bf16[1,8,16,384]{3,2,1,0:T(8,128)(2,1)} %gout_ref.1) | copy-start | bytes 294916

commit v2 on v1

--- a/solution.py
+++ b/solution.py
@@ -11,6 +11,7 @@
 F32, BF16 = jnp.float32, jnp.bfloat16
 LANES = 128
 PIECE = 16
+VMEM_BYTES = 64 * 1024 * 1024
 ORDERS = ("yxz", "xyz", "zyx", "xyz", "yxz", "xyz")
 DIRECTIONS = ((-1, 0), (1, 0), (0, -1), (0, 1), (-1, -1), (-1, 1), (1, -1), (1, 1))
 SIZES = {"y": 2, "x": 2, "z": 4}
@@ -221,17 +222,17 @@
 def fused_kernel(
     sizes,
     scale,
-    x_ref,
-    gout_ref,
-    dwk_ref,
-    dwb_ref,
-    gain_ref,
-    lnb_ref,
+    x_hbm,
+    gout_hbm,
+    dwk_hbm,
+    dwb_hbm,
+    gain_hbm,
+    lnb_hbm,
     wexp_hbm,
-    bexp_ref,
+    bexp_hbm,
     wred_hbm,
-    bred_ref,
-    ls_ref,
+    bred_hbm,
+    ls_hbm,
     out_ref,
     gin_ref,
     gexp_ref,
@@ -239,13 +240,27 @@
     gker_ref,
     gvec_ref,
     gbexp_ref,
+    x_ref,
+    gout_ref,
+    dwk_ref,
+    dwb_1d,
+    gain_1d,
+    lnb_1d,
     wexp,
+    bexp_1d,
     wred,
+    bred_1d,
+    ls_1d,
+    bexp_ref,
+    pre_s,
+    gact_s,
     xp,
     gp,
     work,
     xhat_s,
     lhs_t,
+    act_s,
+    gpre_s,
     main0,
     main1,
     rem,
@@ -282,11 +297,25 @@
     def z_mate(d):
         return {"rows": (z + d) % zn, "cols": x, "rep": r}
 
-    weights = [
-        pltpu.make_async_copy(wexp_hbm, wexp, wsem.at[0]),
-        pltpu.make_async_copy(wred_hbm, wred, wsem.at[1]),
+    fetches = [
+        pltpu.make_async_copy(source, target, wsem.at[n])
+        for n, (source, target) in enumerate(
+            (
+                (x_hbm, x_ref),
+                (gout_hbm, gout_ref),
+                (ls_hbm, ls_1d),
+                (wred_hbm, wred),
+                (dwb_hbm, dwb_1d),
+                (dwk_hbm, dwk_ref),
+                (gain_hbm, gain_1d),
+                (lnb_hbm, lnb_1d),
+                (bexp_hbm, bexp_1d),
+                (bred_hbm, bred_1d),
+                (wexp_hbm, wexp),
+            )
+        )
     ]
-    for copy in weights:
+    for copy in fetches:
         copy.start()
 
     def inside(a, b):
@@ -312,11 +341,13 @@
 
         greeted = greeted + near.astype(jnp.int32)
 
+    xp[...] = jnp.zeros_like(xp)
+    gp[...] = jnp.zeros_like(gp)
+    small[...] = jnp.zeros_like(small)
+    fetches[0].wait()
     cells = x_ref[0].astype(F32)
     for n, (dz, dx) in enumerate(DIRECTIONS):
         xsend[n][...] = halo_source(cells, dz, dx)
-    xp[...] = jnp.zeros_like(xp)
-    gp[...] = jnp.zeros_like(gp)
     xp[3:11, 8:24, :] = cells
     pl.semaphore_wait(barrier, greeted)
 
@@ -350,24 +381,32 @@
             pl.when(inside(z + dz, x + dx))(lambda n=n: halo_copy(which, n).wait_send())
 
     halo_start(0)
+    for copy in fetches[1:10]:
+        copy.wait()
+
+    def row(ref):
+        return ref[...].reshape(1, -1)
+
+    layer_scale, gain = row(ls_1d), row(gain_1d)
+    bexp_ref[...] = row(bexp_1d)
     grad = gout_ref[0].astype(F32).reshape(-1, chans)
-    scaled = grad * ls_ref[...]
+    scaled = grad * layer_scale
     g_branch = scaled.astype(BF16)
-    small[...] = jnp.zeros_like(small)
     small[52:53, :] = jnp.sum(scaled, axis=0, keepdims=True)
-    weights[1].wait()
     contract_last = (((1,), (1,)), ((), ()))
-    g_act = lax.dot_general(g_branch, wred[...], contract_last, preferred_element_type=F32)
+    gact_s[...] = lax.dot_general(g_branch, wred[...], contract_last, preferred_element_type=F32)
     lhs_t[1] = scaled.T.astype(BF16).reshape(rn, chans // rn, 128)
+    bias = row(dwb_1d)
+    work[...] = jnp.broadcast_to(bias, work.shape)
     halo_finish(0, xp)
 
     def conv_chunk(n, carry):
         ch = pl.ds(pl.multiple_of(n * LANES, LANES), LANES)
-        total = jnp.zeros((8, 16, LANES), F32) + dwb_ref[:, ch]
+        total = work[:, ch].reshape(8, 16, LANES)
         for j in range(7):
             shifted = xp[:, 5 + j : 21 + j, ch]
             for i in range(7):
-                total = total + dwk_ref[7 * i + j : 7 * i + j + 1, ch] * shifted[i : i + 8]
+                total = total + dwk_ref[i, j : j + 1, ch] * shifted[i : i + 8]
         work[:, ch] = total.reshape(128, LANES)
         return carry
 
@@ -377,36 +416,50 @@
     rstd = lax.rsqrt(jnp.mean(centered * centered, axis=-1, keepdims=True) + EPS)
     xhat = centered * rstd
     xhat_s[...] = xhat
-    normed32 = xhat * gain_ref[...] + lnb_ref[...]
+    normed32 = xhat * gain + row(lnb_1d)
     normed = normed32.astype(BF16)
     lhs_t[0] = normed32.T.astype(BF16).reshape(rn, chans // rn, 128)
-    weights[0].wait()
-    pre = jnp.dot(normed, wexp[...], preferred_element_type=F32) + bexp_ref[...]
-    cdf = 0.5 * (1.0 + lax.erf(pre * INV_ROOT_TWO))
-    act32 = pre * cdf
-    act = act32.astype(BF16)
-    pdf = jnp.exp(-0.5 * pre * pre) * INV_ROOT_TWO_PI
-    g_pre = g_act * (cdf + pre * pdf)
-    bexp_sum = jnp.sum(g_pre, axis=0, keepdims=True)
+    fetches[10].wait()
+    pre_s[...] = jnp.dot(normed, wexp[...], preferred_element_type=F32)
+
+    lower = lax.broadcasted_iota(jnp.int32, (64, LANES), 1) < LANES // 2
+    zero = jnp.zeros((64, LANES), F32)
+
+    def hidden_pair(n, carry):
+        here = pl.multiple_of(n * 3 * LANES, LANES)
+        even = pl.ds(pl.multiple_of(2 * n * LANES, LANES), LANES)
+        odd = pl.ds(pl.multiple_of(2 * n * LANES + LANES, LANES), LANES)
+        sums = []
+        for group in range(3):
+            ch = pl.ds(pl.multiple_of(here + group * LANES, LANES), LANES)
+            sums.append(jnp.zeros((1, LANES), F32))
+            for top in (0, 64):
+                rows = slice(top, top + 64)
+                after = slice(128 + top, 192 + top)
+                pre = pre_s[rows, ch] + bexp_ref[:, ch]
+                cdf = 0.5 * (1.0 + lax.erf(pre * INV_ROOT_TWO))
+                act = pre * cdf
+                pdf = jnp.exp(-0.5 * pre * pre) * INV_ROOT_TWO_PI
+                g_pre = gact_s[rows, ch] * (cdf + pre * pdf)
+                sums[-1] = sums[-1] + jnp.sum(g_pre, axis=0, keepdims=True)
+                act_s[rows, ch] = act.astype(BF16)
+                gpre_s[rows, ch] = g_pre.astype(BF16)
+                if group == 1:
+                    rolled = pltpu.roll(act, LANES // 2, 1)
+                    rem[rows, even] = jnp.where(lower, g_pre, zero).astype(BF16)
+                    rem[after, even] = jnp.where(lower, zero, rolled).astype(BF16)
+                    rem[rows, odd] = jnp.where(lower, zero, g_pre).astype(BF16)
+                    rem[after, odd] = jnp.where(lower, rolled, zero).astype(BF16)
+                else:
+                    to = odd if group else even
+                    main0[rows, to] = g_pre.astype(BF16)
+                    main1[rows, to] = act.astype(BF16)
+        bexp_ref[:, pl.ds(here, 3 * LANES)] = jnp.concatenate(sums, axis=1)
+        return carry
+
+    lax.fori_loop(0, zn, hidden_pair, 0)
     for n in range(hidden // chans):
-        small[54 + n : 55 + n, :] = bexp_sum[:, n * chans : (n + 1) * chans]
-    g_pre_b = g_pre.astype(BF16)
-
-    low = lax.broadcasted_iota(jnp.int32, (128, LANES), 1) < LANES // 2
-    zero = jnp.zeros((128, LANES), F32)
-    for n in range(zn):
-        at = 3 * LANES * n
-        even, odd = slice(2 * n * LANES, (2 * n + 1) * LANES), slice((2 * n + 1) * LANES, (2 * n + 2) * LANES)
-        main0[:, even] = g_pre_b[:, at : at + LANES]
-        main0[:, odd] = g_pre_b[:, at + 2 * LANES : at + 3 * LANES]
-        main1[:, even] = act[:, at : at + LANES]
-        main1[:, odd] = act[:, at + 2 * LANES : at + 3 * LANES]
-        middle = g_pre[:, at + LANES : at + 2 * LANES]
-        rolled = pltpu.roll(act32[:, at + LANES : at + 2 * LANES], LANES // 2, 1)
-        rem[:128, even] = jnp.where(low, middle, zero).astype(BF16)
-        rem[128:, even] = jnp.where(low, zero, rolled).astype(BF16)
-        rem[:128, odd] = jnp.where(low, zero, middle).astype(BF16)
-        rem[128:, odd] = jnp.where(low, rolled, zero).astype(BF16)
+        small[54 + n : 55 + n, :] = bexp_ref[:, n * chans : (n + 1) * chans]
 
     def products(owner):
         left0 = jnp.concatenate([lhs_t[0, owner], lhs_t[0, 2 + owner]], axis=0)
@@ -501,11 +554,11 @@
     for p in range(parts):
         stage(p, 0)
 
-    g_normed = lax.dot_general(g_pre_b, wexp[...], contract_last, preferred_element_type=F32)
+    g_normed = lax.dot_general(gpre_s[...], wexp[...], contract_last, preferred_element_type=F32)
     xhat = xhat_s[...]
     small[50:51, :] = jnp.sum(g_normed * xhat, axis=0, keepdims=True)
     small[51:52, :] = jnp.sum(g_normed, axis=0, keepdims=True)
-    gx = g_normed * gain_ref[...]
+    gx = g_normed * gain
     g_conv = rstd * (
         gx
         - jnp.mean(gx, axis=-1, keepdims=True)
@@ -517,11 +570,13 @@
         gsend[n][...] = halo_source(g_cells, dz, dx)
     halo_start(1)
     gp[3:11, 8:24, :] = g_cells
-
-    branch = jnp.dot(act, wred[...], preferred_element_type=F32) + bred_ref[...]
+    for p in range(3):
+        stage(p, 1)
+
+    branch = jnp.dot(act_s[...], wred[...], preferred_element_type=F32) + row(bred_1d)
     small[53:54, :] = jnp.sum(grad * branch, axis=0, keepdims=True)
     inner = x_ref[0].astype(F32).reshape(-1, chans)
-    out_ref[0] = (inner + ls_ref[...] * branch).astype(BF16).reshape(8, 16, chans)
+    out_ref[0] = (inner + layer_scale * branch).astype(BF16).reshape(8, 16, chans)
 
     def kernel_chunk(n, carry):
         ch = pl.ds(pl.multiple_of(n * LANES, LANES), LANES)
@@ -554,12 +609,14 @@
     small_send[0] = small[other_rows, :]
     moves[0].start()
 
-    for p in range(parts):
+    for p in range(3, parts):
         stage(p, 1)
 
     moves[0].wait_recv()
     small_send[1] = small[my_rows, :] + small_land[0]
     moves[1].start()
+    for p in range(3):
+        stage(p, 2)
 
     halo_finish(1, gp)
 
@@ -569,7 +626,7 @@
         for j in range(7):
             shifted = gp[:, 11 - j : 27 - j, ch]
             for i in range(7):
-                total = total + dwk_ref[7 * i + j : 7 * i + j + 1, ch] * shifted[6 - i : 14 - i]
+                total = total + dwk_ref[i, j : j + 1, ch] * shifted[6 - i : 14 - i]
         gin_ref[0, :, :, ch] = total.astype(BF16)
         return carry
 
@@ -583,7 +640,7 @@
     for move in z_moves:
         move.start()
 
-    for p in range(parts):
+    for p in range(3, parts):
         stage(p, 2)
 
     for move in z_moves:
@@ -626,7 +683,8 @@
         gker_ref[i] = small[7 * i : 7 * i + 7, :]
     gvec_ref[...] = small[49:54, :]
     for n in range(hidden // chans):
-        gbexp_ref[:, n * chans : (n + 1) * chans] = small[54 + n : 55 + n, :]
+        bexp_ref[:, n * chans : (n + 1) * chans] = small[54 + n : 55 + n, :]
+    gbexp_ref[...] = bexp_ref[...].reshape(-1)
 
     halo_sent(0)
     halo_sent(1)
@@ -659,7 +717,7 @@
     pixels = height * width * zn * xn * rn
     scale = float(pixels) ** -0.5
     vmem = pl.BlockSpec(memory_space=pltpu.VMEM)
-    anywhere = pl.BlockSpec(memory_space=pl.ANY)
+    hbm = pl.BlockSpec(memory_space=pltpu.HBM)
     parts = len(ORDERS)
     block = (3, PIECE, LANES)
     keeps, sends, lands = [], [], []
@@ -675,13 +733,27 @@
             lands[-1].append(pltpu.VMEM((copies,) + left + block, BF16))
     halos = [pltpu.VMEM(halo_shape(dz, dx, chans), BF16) for dz, dx in DIRECTIONS]
     scratch = dict(
+        x_ref=pltpu.VMEM(feature_map.shape, BF16),
+        gout_ref=pltpu.VMEM(cotangent.shape, BF16),
+        dwk_ref=pltpu.VMEM(dw_kernel.shape, F32),
+        dwb_1d=pltpu.VMEM((chans,), F32),
+        gain_1d=pltpu.VMEM((chans,), F32),
+        lnb_1d=pltpu.VMEM((chans,), F32),
         wexp=pltpu.VMEM(w_expand.shape, BF16),
+        bexp_1d=pltpu.VMEM((hidden,), F32),
         wred=pltpu.VMEM(w_reduce.shape, BF16),
+        bred_1d=pltpu.VMEM((chans,), F32),
+        ls_1d=pltpu.VMEM((chans,), F32),
+        bexp_ref=pltpu.VMEM((1, hidden), F32),
+        pre_s=pltpu.VMEM((128, hidden), F32),
+        gact_s=pltpu.VMEM((128, hidden), F32),
         xp=pltpu.VMEM((14, 32, chans), F32),
         gp=pltpu.VMEM((14, 32, chans), F32),
         work=pltpu.VMEM((128, chans), F32),
         xhat_s=pltpu.VMEM((128, chans), F32),
         lhs_t=pltpu.VMEM((2, rn, chans // rn, 128), BF16),
+        act_s=pltpu.VMEM((128, hidden), BF16),
+        gpre_s=pltpu.VMEM((128, hidden), BF16),
         main0=pltpu.VMEM((128, 2 * zn * LANES), BF16),
         main1=pltpu.VMEM((128, 2 * zn * LANES), BF16),
         rem=pltpu.VMEM((256, 2 * zn * LANES), BF16),
@@ -700,7 +772,7 @@
         keeps=keeps,
         sends=sends,
         lands=lands,
-        wsem=pltpu.SemaphoreType.DMA((2,)),
+        wsem=pltpu.SemaphoreType.DMA((11,)),
         halo_sems=pltpu.SemaphoreType.DMA((2, 2, 8)),
         core_sems=pltpu.SemaphoreType.DMA((2, parts)),
         part_sems=pltpu.SemaphoreType.DMA((parts, 3, 2, 3)),
@@ -716,28 +788,47 @@
             jax.ShapeDtypeStruct((rows, columns), F32),
             jax.ShapeDtypeStruct(dw_kernel.shape, F32),
             jax.ShapeDtypeStruct((5, chans), F32),
-            jax.ShapeDtypeStruct((1, hidden), F32),
+            jax.ShapeDtypeStruct((hidden,), F32),
         ],
-        in_specs=[vmem] * 6 + [anywhere, vmem, anywhere, vmem, vmem],
+        in_specs=[hbm] * 11,
         out_specs=[vmem] * 7,
         scratch_shapes=list(scratch.values()),
         compiler_params=pltpu.CompilerParams(
-            collective_id=0, has_side_effects=True, vmem_limit_bytes=48 * 1024 * 1024
+            collective_id=0, has_side_effects=True, vmem_limit_bytes=VMEM_BYTES
         ),
     )(
         feature_map,
         cotangent,
-        dw_kernel.reshape(49, chans),
-        dw_bias.reshape(1, -1),
-        layer_norm_gain.reshape(1, -1),
-        layer_norm_bias.reshape(1, -1),
+        dw_kernel,
+        dw_bias,
+        layer_norm_gain,
+        layer_norm_bias,
         w_expand,
-        b_expand.reshape(1, -1),
+        b_expand,
         w_reduce,
-        b_reduce.reshape(1, -1),
-        layer_scale.reshape(1, -1),
-    )
-    return tuple(outs[:6]) + (outs[6].reshape(-1),)
+        b_reduce,
+        layer_scale,
+    )
+    shapes = [jax.ShapeDtypeStruct(o.shape, o.dtype) for o in outs]
+    return tuple(
+        pl.pallas_call(
+            write_out,
+            out_shape=shapes,
+            in_specs=[hbm] * 7,
+            out_specs=[hbm] * 7,
+            scratch_shapes=[pltpu.SemaphoreType.DMA((7,))],
+            compiler_params=pltpu.CompilerParams(vmem_limit_bytes=VMEM_BYTES),
+        )(*outs)
+    )
+
+
+def write_out(*refs):
+    sems = refs[14]
+    copies = [pltpu.make_async_copy(refs[n], refs[7 + n], sems.at[n]) for n in range(7)]
+    for copy in copies:
+        copy.start()
+    for copy in copies:
+        copy.wait()
 
 
 def fits(sizes):

time: 55.5 us -> 57.7 us (1.040)
  Pallas kernels: 40.6 us -> 56.9 us
  local copies, waits for them, and re-layouts: 13.1 us -> 0 us
  other arithmetic: 0.62 us -> 0 us
    pallas_call x0 -> x1, Pallas kernels: none -> 16.2 us  [fused(): pl.pallas_call(write_out, out_shape=shapes, in_specs=[hbm] * 7, out_specs...]
    unnamed x14 -> x0, local copies, waits for them, and re-layouts: 8.12 us -> none
    reshape x7 -> x0, local copies, waits for them, and re-layouts: 5.02 us -> none  [the longest x1 0.9 us: fused(): dw_kernel.reshape(49, chans)]
    pallas_call x1 -> x0, other arithmetic: 0.62 us -> none  [fused(): pl.pallas_call(functools.partial(fused_kernel, mesh_sizes, scale), out_sh...]
where the time goes in v2:
time: 57.7 us; the launch traced here: 57.6 us
  Pallas kernels  56.9 us (99%)
  between operations  0.64 us (1%)
    pallas_call x1, Pallas kernels, fused(): pl.pallas_call(functools.partial(fused_kernel, mesh_sizes, scale), out_sh...  40.7 us
    pallas_call x1, Pallas kernels, fused(): pl.pallas_call(write_out, out_shape=shapes, in_specs=[hbm] * 7, out_specs...  16.2 us

profile of v2, /device:TPU:0, one launch (start us, length us, event | category | flops | bytes accessed | tf_op | source)
XLA Modules:
  0.0 57.6 jit_solution(14933358990700282763)
XLA Ops:
  0.6 40.7 %shard_map.162 = (bf16[1,8,16,384]{3,2,1,0:T(8,128)(2,1)}, bf16[1,8,16,384]{3,2,1,0:T(8,128)(2,1)}, f32[96,192]{1,0:T(8,128)}, f32[96,192]{1,0:T(8,128)}, f32[7,...) custom-call(bf16[1,8,16,384]{3,2,1,0:T(8,128)(2,1)} %x_hbm.1, bf16[1,8,16,384]{3,2,1,0:T(8,128)(2,1)} %gout_hbm.1, ...), custom_call_target="tpu_custom_call" | custom-call | tf_op jit(solution)/shard_map/pallas_call | solution.py:782
  41.3 16.2 %shard_map.163 = (bf16[1,8,16,384]{3,2,1,0:T(8,128)(2,1)}, bf16[1,8,16,384]{3,2,1,0:T(8,128)(2,1)}, f32[96,192]{1,0:T(8,128)}, f32[96,192]{1,0:T(8,128)}, f32[7,...) custom-call(bf16[1,8,16,384]{3,2,1,0:T(8,128)(2,1)} %get-tuple-element.14.refs_0_, ...), custom_call_target="tpu_custom_call" | custom-call | tf_op jit(solution)/shard_map/pallas_call | solution.py:814

commit v3 on v2

--- a/solution.py
+++ b/solution.py
@@ -10,7 +10,7 @@
 MESH = pl.DeviceIdType.MESH
 F32, BF16 = jnp.float32, jnp.bfloat16
 LANES = 128
-PIECE = 16
+PIECE = 48
 VMEM_BYTES = 64 * 1024 * 1024
 ORDERS = ("yxz", "xyz", "zyx", "xyz", "yxz", "xyz")
 DIRECTIONS = ((-1, 0), (1, 0), (0, -1), (0, 1), (-1, -1), (-1, 1), (1, -1), (1, 1))
@@ -461,20 +461,24 @@
     for n in range(hidden // chans):
         small[54 + n : 55 + n, :] = bexp_ref[:, n * chans : (n + 1) * chans]
 
-    def products(owner):
+    def left_of(owner):
         left0 = jnp.concatenate([lhs_t[0, owner], lhs_t[0, 2 + owner]], axis=0)
         left1 = jnp.concatenate([lhs_t[1, owner], lhs_t[1, 2 + owner]], axis=0)
-        both = jnp.concatenate([left0, left1], axis=1)
-        rows = chans // rn
-        for k, (left, right) in enumerate(((left0, main0), (left1, main1), (both, rem))):
-            for zz in range(zn):
-                block = jnp.dot(
-                    left, right[:, 2 * zz * LANES : (2 * zz + 2) * LANES], preferred_element_type=F32
-                ).astype(BF16)
-                for xx in range(xn):
-                    for yy in range(2):
-                        part = block[yy * rows : (yy + 1) * rows, xx * LANES : (xx + 1) * LANES]
-                        grad_out_blocks[owner, :, yy, xx, zz, k] = part.reshape(-1, PIECE, LANES)
+        return left0, left1, jnp.concatenate([left0, left1], axis=1)
+
+    def products(owner, lefts, k):
+        right = (main0, main1, rem)[k]
+        for zz in range(zn):
+            block = jnp.dot(
+                lefts[k], right[:, 2 * zz * LANES : (2 * zz + 2) * LANES], preferred_element_type=F32
+            ).astype(BF16)
+            for xx in range(xn):
+                for yy in range(2):
+                    for h in range(2):
+                        at = (2 * yy + h) * PIECE
+                        grad_out_blocks[owner, 2 * k + h, yy, xx, zz] = block[
+                            at : at + PIECE, xx * LANES : (xx + 1) * LANES
+                        ]
 
     def core_copy(p):
         return pltpu.make_async_remote_copy(
@@ -487,10 +491,11 @@
         )
 
     parts = len(ORDERS)
-    products(1 - c)
-    for p in range(parts):
-        core_copy(p).start()
-    products(c)
+    lefts = left_of(1 - c)
+    for k in range(3):
+        products(1 - c, lefts, k)
+        core_copy(2 * k).start()
+        core_copy(2 * k + 1).start()
 
     def place(dims, axis, index):
         return tuple(index if d == axis else slice(None) for d in dims)
@@ -536,7 +541,7 @@
                 copy.wait_recv()
         dims = [d for d in "yxz" if d not in ORDERS[p][:s]]
         if s == 3:
-            final[:, p * PIECE : (p + 1) * PIECE, :] = load(p, s, ())
+            final[p // 2, (p % 2) * PIECE : (p % 2 + 1) * PIECE, :] = load(p, s, ())
             return
         axis = ORDERS[p][s]
         copies = stage_copies(p, s)
@@ -551,8 +556,11 @@
             copies[0].start()
             keeps[p][s][...] = load(p, s, place(dims, axis, mine))
 
-    for p in range(parts):
-        stage(p, 0)
+    lefts = left_of(c)
+    for k in range(3):
+        products(c, lefts, k)
+        stage(2 * k, 0)
+        stage(2 * k + 1, 0)
 
     g_normed = lax.dot_general(gpre_s[...], wexp[...], contract_last, preferred_element_type=F32)
     xhat = xhat_s[...]
@@ -570,13 +578,14 @@
         gsend[n][...] = halo_source(g_cells, dz, dx)
     halo_start(1)
     gp[3:11, 8:24, :] = g_cells
-    for p in range(3):
-        stage(p, 1)
 
     branch = jnp.dot(act_s[...], wred[...], preferred_element_type=F32) + row(bred_1d)
     small[53:54, :] = jnp.sum(grad * branch, axis=0, keepdims=True)
     inner = x_ref[0].astype(F32).reshape(-1, chans)
     out_ref[0] = (inner + layer_scale * branch).astype(BF16).reshape(8, 16, chans)
+
+    for p in range(3):
+        stage(p, 1)
 
     def kernel_chunk(n, carry):
         ch = pl.ds(pl.multiple_of(n * LANES, LANES), LANES)
@@ -617,6 +626,15 @@
     moves[1].start()
     for p in range(3):
         stage(p, 2)
+    moves[1].wait_recv()
+    small_send[2] = small_send[1] + small_land[1]
+    moves[2].start()
+    for p in range(3, parts):
+        stage(p, 2)
+    moves[2].wait_recv()
+    zsend[...] = (small_send[2] + small_land[2]).astype(BF16)
+    for move in z_moves:
+        move.start()
 
     halo_finish(1, gp)
 
@@ -630,18 +648,7 @@
         gin_ref[0, :, :, ch] = total.astype(BF16)
         return carry
 
-    moves[1].wait_recv()
-    small_send[2] = small_send[1] + small_land[1]
-    moves[2].start()
     lax.fori_loop(0, chans // LANES, input_chunk, 0)
-
-    moves[2].wait_recv()
-    zsend[...] = (small_send[2] + small_land[2]).astype(BF16)
-    for move in z_moves:
-        move.start()
-
-    for p in range(3, parts):
-        stage(p, 2)
 
     for move in z_moves:
         move.wait_recv()
@@ -719,7 +726,7 @@
     vmem = pl.BlockSpec(memory_space=pltpu.VMEM)
     hbm = pl.BlockSpec(memory_space=pltpu.HBM)
     parts = len(ORDERS)
-    block = (3, PIECE, LANES)
+    block = (PIECE, LANES)
     keeps, sends, lands = [], [], []
     for order in ORDERS:
         keeps.append([])
@@ -768,7 +775,7 @@
         small_land=pltpu.VMEM((4, 32, chans), F32),
         zsend=pltpu.VMEM((32, chans), BF16),
         zland=pltpu.VMEM((3, 32, chans), BF16),
-        final=pltpu.VMEM((3, parts * PIECE, LANES), F32),
+        final=pltpu.VMEM((3, 2 * PIECE, LANES), F32),
         keeps=keeps,
         sends=sends,
         lands=lands,
@@ -816,18 +823,23 @@
             out_shape=shapes,
             in_specs=[hbm] * 7,
             out_specs=[hbm] * 7,
-            scratch_shapes=[pltpu.SemaphoreType.DMA((7,))],
+            scratch_shapes=[pltpu.VMEM(o.shape, o.dtype) for o in outs]
+            + [pltpu.SemaphoreType.DMA((2, 7))],
             compiler_params=pltpu.CompilerParams(vmem_limit_bytes=VMEM_BYTES),
         )(*outs)
     )
 
 
 def write_out(*refs):
-    sems = refs[14]
-    copies = [pltpu.make_async_copy(refs[n], refs[7 + n], sems.at[n]) for n in range(7)]
-    for copy in copies:
+    sems = refs[21]
+    reads = [pltpu.make_async_copy(refs[n], refs[14 + n], sems.at[0, n]) for n in range(7)]
+    writes = [pltpu.make_async_copy(refs[14 + n], refs[7 + n], sems.at[1, n]) for n in range(7)]
+    for copy in reads:
         copy.start()
-    for copy in copies:
+    for read, write in zip(reads, writes):
+        read.wait()
+        write.start()
+    for copy in writes:
         copy.wait()
 
 

time: 57.7 us -> 41.2 us (0.71)
  Pallas kernels: 56.9 us -> 40.4 us
    pallas_call x1, Pallas kernels: 16.2 us -> 1.84 us  [fused(): pl.pallas_call(write_out, out_shape=shapes, in_specs=[hbm] * 7, out_specs...]
    pallas_call x1, Pallas kernels: 40.7 us -> 38.5 us  [fused(): pl.pallas_call(functools.partial(fused_kernel, mesh_sizes, scale), out_sh...]
where the time goes in v3:
time: 41.2 us; the launch traced here: 41 us
  Pallas kernels  40.4 us (98%)
  between operations  0.64 us (2%)
    pallas_call x1, Pallas kernels, fused(): pl.pallas_call(functools.partial(fused_kernel, mesh_sizes, scale), out_sh...  38.5 us
    pallas_call x1, Pallas kernels, fused(): pl.pallas_call(write_out, out_shape=shapes, in_specs=[hbm] * 7, out_specs...  1.84 us

profile of v3, /device:TPU:0, one launch (start us, length us, event | category | flops | bytes accessed | tf_op | source)
XLA Modules:
  0.0 41.0 jit_solution(3722251523515390934)
XLA Ops:
  0.6 38.5 %shard_map.162 = (bf16[1,8,16,384]{3,2,1,0:T(8,128)(2,1)}, bf16[1,8,16,384]{3,2,1,0:T(8,128)(2,1)}, f32[96,192]{1,0:T(8,128)}, f32[96,192]{1,0:T(8,128)}, f32[7,...) custom-call(bf16[1,8,16,384]{3,2,1,0:T(8,128)(2,1)} %x_hbm.1, bf16[1,8,16,384]{3,2,1,0:T(8,128)(2,1)} %gout_hbm.1, ...), custom_call_target="tpu_custom_call" | custom-call | tf_op jit(solution)/shard_map/pallas_call | solution.py:789
  39.2 1.8 %shard_map.163 = (bf16[1,8,16,384]{3,2,1,0:T(8,128)(2,1)}, bf16[1,8,16,384]{3,2,1,0:T(8,128)(2,1)}, f32[96,192]{1,0:T(8,128)}, f32[96,192]{1,0:T(8,128)}, f32[7,...) custom-call(bf16[1,8,16,384]{3,2,1,0:T(8,128)(2,1)} %get-tuple-element.14.refs_0_, ...), custom_call_target="tpu_custom_call" | custom-call | tf_op jit(solution)/shard_map/pallas_call | solution.py:821

commit v4 on v3

--- a/solution.py
+++ b/solution.py
@@ -420,18 +420,26 @@
     normed = normed32.astype(BF16)
     lhs_t[0] = normed32.T.astype(BF16).reshape(rn, chans // rn, 128)
     fetches[10].wait()
-    pre_s[...] = jnp.dot(normed, wexp[...], preferred_element_type=F32)
+    lefts_of = {}
+    for owner, name in ((1 - c, "mate"), (c, "own")):
+        left0 = jnp.concatenate([lhs_t[0, owner], lhs_t[0, 2 + owner]], axis=0)
+        left1 = jnp.concatenate([lhs_t[1, owner], lhs_t[1, 2 + owner]], axis=0)
+        lefts_of[name] = (left0, left1, jnp.concatenate([left0, left1], axis=1))
+
+    def expand_group(n):
+        at = slice(n * 3 * LANES, (n + 1) * 3 * LANES)
+        pre_s[:, at] = jnp.dot(normed, wexp[:, at], preferred_element_type=F32)
 
     lower = lax.broadcasted_iota(jnp.int32, (64, LANES), 1) < LANES // 2
     zero = jnp.zeros((64, LANES), F32)
 
-    def hidden_pair(n, carry):
-        here = pl.multiple_of(n * 3 * LANES, LANES)
-        even = pl.ds(pl.multiple_of(2 * n * LANES, LANES), LANES)
-        odd = pl.ds(pl.multiple_of(2 * n * LANES + LANES, LANES), LANES)
+    def hidden_pair(n):
+        here = n * 3 * LANES
+        even = slice(2 * n * LANES, (2 * n + 1) * LANES)
+        odd = slice((2 * n + 1) * LANES, (2 * n + 2) * LANES)
         sums = []
         for group in range(3):
-            ch = pl.ds(pl.multiple_of(here + group * LANES, LANES), LANES)
+            ch = slice(here + group * LANES, here + (group + 1) * LANES)
             sums.append(jnp.zeros((1, LANES), F32))
             for top in (0, 64):
                 rows = slice(top, top + 64)
@@ -454,21 +462,10 @@
                     to = odd if group else even
                     main0[rows, to] = g_pre.astype(BF16)
                     main1[rows, to] = act.astype(BF16)
-        bexp_ref[:, pl.ds(here, 3 * LANES)] = jnp.concatenate(sums, axis=1)
-        return carry
-
-    lax.fori_loop(0, zn, hidden_pair, 0)
-    for n in range(hidden // chans):
-        small[54 + n : 55 + n, :] = bexp_ref[:, n * chans : (n + 1) * chans]
-
-    def left_of(owner):
-        left0 = jnp.concatenate([lhs_t[0, owner], lhs_t[0, 2 + owner]], axis=0)
-        left1 = jnp.concatenate([lhs_t[1, owner], lhs_t[1, 2 + owner]], axis=0)
-        return left0, left1, jnp.concatenate([left0, left1], axis=1)
-
-    def products(owner, lefts, k):
-        right = (main0, main1, rem)[k]
-        for zz in range(zn):
+        small[54 + n : 55 + n, :] = jnp.concatenate(sums, axis=1)
+
+    def products(owner, lefts, zz):
+        for k, right in enumerate((main0, main1, rem)):
             block = jnp.dot(
                 lefts[k], right[:, 2 * zz * LANES : (2 * zz + 2) * LANES], preferred_element_type=F32
             ).astype(BF16)
@@ -480,22 +477,28 @@
                             at : at + PIECE, xx * LANES : (xx + 1) * LANES
                         ]
 
-    def core_copy(p):
+    def core_copy(zz):
         return pltpu.make_async_remote_copy(
-            src_ref=grad_out_blocks.at[1 - c, p],
-            dst_ref=landed0.at[p],
-            send_sem=core_sems.at[0, p],
-            recv_sem=core_sems.at[1, p],
+            src_ref=grad_out_blocks.at[1 - c, :, :, :, zz],
+            dst_ref=landed0.at[:, :, :, zz],
+            send_sem=core_sems.at[0, zz],
+            recv_sem=core_sems.at[1, zz],
             device_id=core_mate,
             device_id_type=MESH,
         )
 
     parts = len(ORDERS)
-    lefts = left_of(1 - c)
-    for k in range(3):
-        products(1 - c, lefts, k)
-        core_copy(2 * k).start()
-        core_copy(2 * k + 1).start()
+    expand_group(0)
+    expand_group(1)
+    hidden_pair(0)
+    for n in range(zn):
+        products(1 - c, lefts_of["mate"], n)
+        products(c, lefts_of["own"], n)
+        if n + 2 < zn:
+            expand_group(n + 2)
+        if n + 1 < zn:
+            hidden_pair(n + 1)
+        core_copy(n).start()
 
     def place(dims, axis, index):
         return tuple(index if d == axis else slice(None) for d in dims)
@@ -534,9 +537,7 @@
         return total
 
     def stage(p, s):
-        if s == 0:
-            core_copy(p).wait_recv()
-        else:
+        if s:
             for copy in stage_copies(p, s - 1):
                 copy.wait_recv()
         dims = [d for d in "yxz" if d not in ORDERS[p][:s]]
@@ -556,11 +557,10 @@
             copies[0].start()
             keeps[p][s][...] = load(p, s, place(dims, axis, mine))
 
-    lefts = left_of(c)
-    for k in range(3):
-        products(c, lefts, k)
-        stage(2 * k, 0)
-        stage(2 * k + 1, 0)
+    for n in range(zn):
+        core_copy(n).wait_recv()
+    for p in range(parts):
+        stage(p, 0)
 
     g_normed = lax.dot_general(gpre_s[...], wexp[...], contract_last, preferred_element_type=F32)
     xhat = xhat_s[...]
@@ -695,8 +695,9 @@
 
     halo_sent(0)
     halo_sent(1)
+    for n in range(zn):
+        core_copy(n).wait_send()
     for p in range(parts):
-        core_copy(p).wait_send()
         for s in range(3):
             for copy in stage_copies(p, s):
                 copy.wait_send()
@@ -781,7 +782,7 @@
         lands=lands,
         wsem=pltpu.SemaphoreType.DMA((11,)),
         halo_sems=pltpu.SemaphoreType.DMA((2, 2, 8)),
-        core_sems=pltpu.SemaphoreType.DMA((2, parts)),
+        core_sems=pltpu.SemaphoreType.DMA((2, zn)),
         part_sems=pltpu.SemaphoreType.DMA((parts, 3, 2, 3)),
         small_sems=pltpu.SemaphoreType.DMA((2, 7)),
     )

time: 41.2 us -> 39.9 us (0.968)
  Pallas kernels: 40.4 us -> 39 us
    pallas_call x1, Pallas kernels: 38.5 us -> 37.2 us  [fused(): pl.pallas_call(functools.partial(fused_kernel, mesh_sizes, scale), out_sh...]
where the time goes in v4:
time: 39.9 us; the launch traced here: 39.7 us
  Pallas kernels  39 us (98%)
  between operations  0.64 us (2%)
    pallas_call x1, Pallas kernels, fused(): pl.pallas_call(functools.partial(fused_kernel, mesh_sizes, scale), out_sh...  37.2 us
    pallas_call x1, Pallas kernels, fused(): pl.pallas_call(write_out, out_shape=shapes, in_specs=[hbm] * 7, out_specs...  1.84 us

profile of v4, /device:TPU:0, one launch (start us, length us, event | category | flops | bytes accessed | tf_op | source)
XLA Modules:
  0.0 39.7 jit_solution(6474584569407686486)
XLA Ops:
  0.6 37.2 %shard_map.162 = (bf16[1,8,16,384]{3,2,1,0:T(8,128)(2,1)}, bf16[1,8,16,384]{3,2,1,0:T(8,128)(2,1)}, f32[96,192]{1,0:T(8,128)}, f32[96,192]{1,0:T(8,128)}, f32[7,...) custom-call(bf16[1,8,16,384]{3,2,1,0:T(8,128)(2,1)} %x_hbm.1, bf16[1,8,16,384]{3,2,1,0:T(8,128)(2,1)} %gout_hbm.1, ...), custom_call_target="tpu_custom_call" | custom-call | tf_op jit(solution)/shard_map/pallas_call | solution.py:790
  37.8 1.8 %shard_map.163 = (bf16[1,8,16,384]{3,2,1,0:T(8,128)(2,1)}, bf16[1,8,16,384]{3,2,1,0:T(8,128)(2,1)}, f32[96,192]{1,0:T(8,128)}, f32[96,192]{1,0:T(8,128)}, f32[7,...) custom-call(bf16[1,8,16,384]{3,2,1,0:T(8,128)(2,1)} %get-tuple-element.14.refs_0_, ...), custom_call_target="tpu_custom_call" | custom-call | tf_op jit(solution)/shard_map/pallas_call | solution.py:822

commit v5 on v4

--- a/solution.py
+++ b/solution.py
@@ -578,14 +578,15 @@
         gsend[n][...] = halo_source(g_cells, dz, dx)
     halo_start(1)
     gp[3:11, 8:24, :] = g_cells
+    stage(0, 1)
+    stage(1, 1)
 
     branch = jnp.dot(act_s[...], wred[...], preferred_element_type=F32) + row(bred_1d)
     small[53:54, :] = jnp.sum(grad * branch, axis=0, keepdims=True)
     inner = x_ref[0].astype(F32).reshape(-1, chans)
     out_ref[0] = (inner + layer_scale * branch).astype(BF16).reshape(8, 16, chans)
 
-    for p in range(3):
-        stage(p, 1)
+    stage(2, 1)
 
     def kernel_chunk(n, carry):
         ch = pl.ds(pl.multiple_of(n * LANES, LANES), LANES)

time: 39.9 us -> 39.9 us (level)
  no operation moved by 1% of the time
where the time goes in v5:
time: 39.9 us; the launch traced here: 39.7 us
  Pallas kernels  39 us (98%)
  between operations  0.64 us (2%)
    pallas_call x1, Pallas kernels, fused(): pl.pallas_call(functools.partial(fused_kernel, mesh_sizes, scale), out_sh...  37.2 us
    pallas_call x1, Pallas kernels, fused(): pl.pallas_call(write_out, out_shape=shapes, in_specs=[hbm] * 7, out_specs...  1.84 us

profile of v5, /device:TPU:0, one launch (start us, length us, event | category | flops | bytes accessed | tf_op | source)
XLA Modules:
  0.0 39.7 jit_solution(16055058286270076768)
XLA Ops:
  0.6 37.2 %shard_map.162 = (bf16[1,8,16,384]{3,2,1,0:T(8,128)(2,1)}, bf16[1,8,16,384]{3,2,1,0:T(8,128)(2,1)}, f32[96,192]{1,0:T(8,128)}, f32[96,192]{1,0:T(8,128)}, f32[7,...) custom-call(bf16[1,8,16,384]{3,2,1,0:T(8,128)(2,1)} %x_hbm.1, bf16[1,8,16,384]{3,2,1,0:T(8,128)(2,1)} %gout_hbm.1, ...), custom_call_target="tpu_custom_call" | custom-call | tf_op jit(solution)/shard_map/pallas_call | solution.py:791
  37.8 1.8 %shard_map.163 = (bf16[1,8,16,384]{3,2,1,0:T(8,128)(2,1)}, bf16[1,8,16,384]{3,2,1,0:T(8,128)(2,1)}, f32[96,192]{1,0:T(8,128)}, f32[96,192]{1,0:T(8,128)}, f32[7,...) custom-call(bf16[1,8,16,384]{3,2,1,0:T(8,128)(2,1)} %get-tuple-element.14.refs_0_, ...), custom_call_target="tpu_custom_call" | custom-call | tf_op jit(solution)/shard_map/pallas_call | solution.py:823
